TPU v7x, 128 devices: a whole 4x4x4 slice. The times are simulated.
128 devices in a mesh: dp: 16 (over x, z_hi, core), fsdp: 8 (over z_lo, y).
Axes of the slice: x: 4, y: 4, z: 4 (z_hi: 2, z_lo: 2; z = z_hi * 2 + z_lo), core: 2. Of those that a mesh axis runs over, the one named last changes fastest.
Arguments:
- activations: bfloat16 [16384, 8192], P(('dp', 'fsdp')), may hold values from -24 to 24
- gate_cotangent: bfloat16 [16384, 28672], P(('dp', 'fsdp')), may hold values from -24 to 24
- up_cotangent: bfloat16 [16384, 28672], P(('dp', 'fsdp')), may hold values from -24 to 24
- seeds: int32 [2], replicated, may hold values from 0 to 999999
- gate_first: float32 [8192, 128], P('fsdp'), may hold values from -1.2 to 1.2
- gate_second: float32 [8192, 128], P('fsdp'), may hold values from 0.005 to 0.05
- up_first: float32 [8192, 128], P('fsdp'), may hold values from -1.2 to 1.2
- up_second: float32 [8192, 128], P('fsdp'), may hold values from 0.005 to 0.05
Outputs:
- gate_step: bfloat16 [8192, 28672], P('fsdp', 'dp')
- up_step: bfloat16 [8192, 28672], P('fsdp', 'dp')
- gate_first_new: float32 [8192, 128], P('fsdp')
- gate_second_new: float32 [8192, 128], P('fsdp')
- up_first_new: float32 [8192, 128], P('fsdp')
- up_second_new: float32 [8192, 128], P('fsdp')
Inputs may be any that keep to these rules, and one draw needn't show every extreme that they name: seeds[0] is the gate projection's seed, seeds[1] the up projection's.
All inputs are finite; a program needn't handle non-finite values.
Results may differ from a plain program's by a relative error of at most 0.0063.
Values sent between devices are 32-bit elements; how exact they have to be, the bound alone decides.
No kernel may reach another device: no remote copies, remote signals or barrier semaphores. Data moves between devices by JAX's collectives and lax.ppermute only.
A program may use at most 128 MiB of HBM per device.

v0:
```python
import math

import jax
import jax.numpy as jnp
from jax import lax
from jax.sharding import PartitionSpec as P

FF = 28672
R = 128


beta_one = 0.9
beta_two = 0.95
bias_one = 1.0 - beta_one**10
bias_two = 1.0 - beta_two**10
epsilon = 1e-08


def projection(seed_value, rows, rank):
    index = lax.broadcasted_iota(jnp.int32, (rows, rank), 0) * rank + lax.broadcasted_iota(
        jnp.int32, (rows, rank), 1
    )
    mixed = jnp.bitwise_xor(index, seed_value)
    mixed = mixed * 668265261
    mixed = jnp.bitwise_xor(mixed, jnp.right_shift(mixed, 15) & 131071)
    mixed = mixed * 739982445
    mixed = jnp.bitwise_xor(mixed, jnp.right_shift(mixed, 12) & 1048575)
    level = jnp.right_shift(mixed, 8) & 65535
    unit = (level.astype(jnp.float32) + 0.5) * (2.0 / 65536.0) - 1.0
    return (unit * math.sqrt(3.0 / rank)).astype(jnp.bfloat16)


def contract_rows(left, right):
    return lax.dot_general(
        left, right, (((0,), (0,)), ((), ())), preferred_element_type=jnp.float32
    )


def moments_update(grad, first, second):
    first_new = beta_one * first + (1.0 - beta_one) * grad
    second_new = beta_two * second + (1.0 - beta_two) * grad * grad
    return (first_new, second_new)


def back_project(direction, basis_rows):
    return lax.dot_general(
        direction, basis_rows, (((1,), (1,)), ((), ())), preferred_element_type=jnp.float32
    ).astype(jnp.bfloat16)


def local(
    activations, gate_cotangent, up_cotangent, seeds, gate_first, gate_second, up_first, up_second
):
    gate_basis = projection(seeds[0], FF, R)
    up_basis = projection(seeds[1], FF, R)
    gate_reduced = jnp.dot(gate_cotangent, gate_basis, preferred_element_type=jnp.float32).astype(
        jnp.bfloat16
    )
    up_reduced = jnp.dot(up_cotangent, up_basis, preferred_element_type=jnp.float32).astype(
        jnp.bfloat16
    )
    reduced = jnp.concatenate([gate_reduced, up_reduced], axis=1)
    first_both = jnp.concatenate([gate_first, up_first], axis=1)
    second_both = jnp.concatenate([gate_second, up_second], axis=1)
    dp_count = lax.axis_size("dp")
    fsdp_count = lax.axis_size("fsdp")
    tok_rows = activations.shape[0]
    tokens_all = tok_rows * dp_count * fsdp_count
    whole = contract_rows(activations, reduced)
    whole = lax.psum(whole, "dp")
    summed = lax.psum_scatter(whole, "fsdp", scatter_dimension=0, tiled=True)
    first_new, second_new = moments_update(summed / tokens_all, first_both, second_both)
    direction = (first_new / bias_one / (jnp.sqrt(second_new / bias_two) + epsilon)).astype(
        jnp.bfloat16
    )
    column_count = FF // dp_count
    column_start = lax.axis_index("dp") * column_count
    gate_rows = lax.dynamic_slice_in_dim(gate_basis, column_start, column_count, 0)
    up_rows = lax.dynamic_slice_in_dim(up_basis, column_start, column_count, 0)
    gate_step = back_project(direction[:, :R], gate_rows)
    up_step = back_project(direction[:, R:], up_rows)
    return (
        gate_step,
        up_step,
        first_new[:, :R],
        second_new[:, :R],
        first_new[:, R:],
        second_new[:, R:],
    )


def solution(mesh):
    placed = (
        P(("dp", "fsdp"), None),
        P(("dp", "fsdp"), None),
        P(("dp", "fsdp"), None),
        P(),
        P("fsdp", None),
        P("fsdp", None),
        P("fsdp", None),
        P("fsdp", None),
    )
    return jax.shard_map(
        local,
        mesh=mesh,
        in_specs=placed,
        out_specs=(
            P("fsdp", "dp"),
            P("fsdp", "dp"),
            P("fsdp", None),
            P("fsdp", None),
            P("fsdp", None),
            P("fsdp", None),
        ),
        check_vma=False,
    )
```

profile of v0, /device:TPU:1, one launch (start us, length us, event | category | flops | bytes accessed | tf_op | source)
XLA Modules:
  0.0 310.6 jit_solution(6947423659183995697)
XLA Ops:
  7.2 0.0 copy-start
  7.2 0.0 reduce-scatter.2.cloned.1.call-start
  7.2 1.4 fusion.46
  8.6 17.2 %fusion.4 = bf16[128,128]{0,1:T(8,128)(2,1)S(1)} fusion(bf16[128,28672]{1,0:T(8,128)(2,1)} %param.9, s32[]{:T(128)} %bitcast, s32[28672]{0:T(1024)S(1)} %iota_multiply_fusion), kind=kOutput, calls=%fused_computation.10 | convolution fusion | flops 1005600768 | bytes 7487492 | tf_op jit(solution)/shard_map/dot_general | solution.py:56
  25.9 17.1 %fusion.5 = bf16[128,128]{0,1:T(8,128)(2,1)S(1)} fusion(bf16[128,28672]{1,0:T(8,128)(2,1)S(1)} %copy-done.2, s32[]{:T(128)} %bitcast.2, s32[28672]{0:T(1024)S(1)} %iota_multiply_fusion), kind=kOutput, calls=%fused_computation.11 | convolution fusion | flops 1005600768 | bytes 7487492 | tf_op jit(solution)/shard_map/dot_general | solution.py:59
  42.9 4.5 %convolution_bitcast_fusion = f32[8192,256]{0,1:T(8,128)} fusion(bf16[128,8192]{1,0:T(8,128)(2,1)S(1)} %copy-done, bf16[128,128]{0,1:T(8,128)(2,1)S(1)} %fusion.5, bf16[128,128]{0,1:T(8,128)(2,1)S(1)} %fusion.4), kind=kOutput, calls=%fused_computation.3 | convolution fusion | flops 537001984 | bytes 10551296 | tf_op jit(solution)/shard_map/dot_general | solution.py:34
  47.4 0.0 reduce-scatter.2.cloned.1.call-update
  47.4 0.0 all-reduce.2.cloned.1.call-start
  47.5 96.1 %reduce-scatter.2.cloned.1.call-done = f32[1024,256]{0,1:T(8,128)} async-done(((f32[8192,256]{0,1:T(8,128)}), f32[1024,256]{0,1:T(8,128)}) %reduce-scatter.2.cloned.1.call-update) | async-done | bytes 1048592 | tf_op jit(solution)/shard_map/reduce_scatter | solution.py:71
  143.6 0.0 all-reduce.2.cloned.1.call-update
  143.6 22.4 %multiply_convert_fusion = (bf16[28672,128]{1,0:T(8,128)(2,1)}, bf16[28672,128]{1,0:T(8,128)(2,1)}) fusion(s32[]{:T(128)} %bitcast.2, s32[28672]{0:T(1024)S(1)} %iota_multiply_fusion, s32[]{:T(128)} %bitcast), kind=kLoop, calls=%fused_computation | loop fusion | flops 128450560 | bytes 14794760 | tf_op jit(solution)/shard_map/convert_element_type | solution.py:30
  166.0 0.2 copy.14
  166.2 2.0 copy.16
  168.2 2.0 copy.15
  170.3 2.0 copy.17
  172.3 112.8 %all-reduce.2.cloned.1.call-done = f32[1024,256]{0,1:T(8,128)} async-done(((f32[1024,256]{0,1:T(8,128)}), f32[1024,256]{0,1:T(8,128)}) %all-reduce.2.cloned.1.call-update) | async-done | bytes 1048592 | tf_op jit(solution)/shard_map/psum | solution.py:70
  285.1 2.4 divide_convert_fusion
  287.4 1.2 fusion.44
  288.6 2.0 copy.21
  290.7 2.0 copy.19
  292.7 2.0 copy.18
  294.7 1.0 copy.20
  295.7 4.0 %convolution_convert_fusion = bf16[1024,1792]{1,0:T(8,128)(2,1)} fusion(bf16[28672,128]{1,0:T(8,128)(2,1)} %get-tuple-element.19, s32[]{:T(128)S(6)} %select_n.4, bf16[1024,256]{0,1:T(8,128)(2,1)S(1)} %get-tuple-element.12), kind=kOutput, calls=%fused_computation.4 | convolution fusion | flops 471597056 | bytes 4390916 | tf_op jit(solution)/shard_map/dot_general | solution.py:46
  299.7 4.0 %convolution_convert_fusion.1 = bf16[1024,1792]{1,0:T(8,128)(2,1)} fusion(bf16[28672,128]{1,0:T(8,128)(2,1)} %get-tuple-element.20, s32[]{:T(128)S(6)} %select_n.4, bf16[1024,256]{0,1:T(8,128)(2,1)S(1)} %get-tuple-element.12), kind=kOutput, calls=%fused_computation.5 | convolution fusion | flops 471597056 | bytes 4390916 | tf_op jit(solution)/shard_map/dot_general | solution.py:46
  (6 shorter events, 0.0 us)
Async XLA Ops:
  7.2 35.8 %copy-start = (bf16[128,8192]{1,0:T(8,128)(2,1)S(1)}, bf16[128,8192]{1,0:T(8,128)(2,1)}, u32[]{:S(2)}) copy-start(bf16[128,8192]{1,0:T(8,128)(2,1)} %param.8) | copy-start | bytes 6291460
  7.2 136.4 %reduce-scatter.2.cloned.1.call-start = ((), (), s32[]{:S(2)}) async-start(), calls=%async_computation.1 | async-start | bytes 9437184 | tf_op jit(solution)/shard_map/reduce_scatter | solution.py:71
  8.6 17.2 %copy-start.2 = (bf16[128,28672]{1,0:T(8,128)(2,1)S(1)}, bf16[128,28672]{1,0:T(8,128)(2,1)}, u32[]{:S(2)}) copy-start(bf16[128,28672]{1,0:T(8,128)(2,1)} %param.10) | copy-start | bytes 22020100
  47.4 118.6 %copy-start.1 = (f32[1024,128]{1,0:T(8,128)S(1)}, f32[1024,128]{1,0:T(8,128)}, u32[]{:S(2)}) copy-start(f32[1024,128]{1,0:T(8,128)} %param.12) | copy-start | bytes 1572868
  47.4 237.6 %all-reduce.2.cloned.1.call-start = ((), (), s32[]{:S(2)}) async-start(), calls=%async_computation.2 | async-start | bytes 2097152 | tf_op jit(solution)/shard_map/psum | solution.py:70
Sparse Core Ops, SparseCore 0:
  47.6 96.0 reduce-scatter.1
  146.1 138.9 all-reduce.1
where the time goes:
time: 311 us
  waiting for transfers between devices  209 us (67%)
  matrix products  46.7 us (15%)
  other arithmetic  24.7 us (8%)
  local copies, waits for them, and re-layouts  16 us (5%)
  between operations  14.1 us (5%)
    psum x1, waiting for transfers between devices, local(): whole = lax.psum(whole, 'dp')  113 us
    reduce_scatter x1, waiting for transfers between devices, local(): summed = lax.psum_scatter(whole, 'fsdp', scatter_dimension=0, tiled=True)  96.1 us
    convert_element_type x1, other arithmetic, projection(): return (unit * math.sqrt(3.0 / rank)).astype(jnp.bfloat16)  22.4 us
    dot_general x1, matrix products, local(): jnp.dot(gate_cotangent, gate_basis, preferred_element_type=jnp.float32)  17.2 us
    dot_general x1, matrix products, local(): jnp.dot(up_cotangent, up_basis, preferred_element_type=jnp.float32)  17.1 us
    unnamed x14, local copies, waits for them, and re-layouts  13.4 us
    dot_general x2, matrix products, back_project(): lax.dot_general(direction, basis_rows, (((1,), (1,)), ((), ())), preferre...  8 us
  transfers between devices with their start and end apart: 2, of which 2 were waited for; matrix products, arithmetic and copies ran while one was open for 9% of the time, Pallas kernels for 0%

commit v1 on v0

v1 whole, which is shorter than its diff:
```python
import functools
import math

import jax
import jax.numpy as jnp
import numpy as np
from jax import lax
from jax.experimental import pallas as pl
from jax.experimental.pallas import tpu as pltpu
from jax.sharding import Mesh
from jax.sharding import PartitionSpec as P

FF = 28672
R = 128
TOKENS = 16384

beta_one = 0.9
beta_two = 0.95
bias_one = 1.0 - beta_one**10
bias_two = 1.0 - beta_two**10
epsilon = 1e-08

MIX_ONE = 668265261
MIX_TWO = 739982445
CENTRE = 32767.5 * 256.0
SCALE = float(np.float32(math.sqrt(3.0 / R))) * 2.0**-23

AXES = ("x", "zh", "core", "zl", "y")
SIZES = (4, 2, 2, 2, 4)

BF16 = jnp.bfloat16
F32 = jnp.float32


def finish(mixed):
    mixed = mixed ^ lax.shift_right_logical(mixed, 15)
    mixed = mixed * jnp.int32(MIX_TWO)
    mixed = mixed ^ lax.shift_right_logical(mixed, 12)
    level = (mixed & 0x00FFFF00).astype(F32)
    return ((level - CENTRE) * SCALE).astype(BF16)


def first_mix(local, low, seed):
    return (local ^ (seed & low)) * jnp.int32(MIX_ONE)


def base_mix(base, low, seed):
    return (base ^ (seed & ~low)) * jnp.int32(MIX_ONE)


CHUNK = 2048
TILE = 64
PIECE = 512


def reduce_kernel(
    seed_ref, gate_hbm, up_hbm, out_ref, gate_v, up_v, even, odd, acc, sems
):
    chunks = FF // CHUNK
    hbm = (gate_hbm, up_hbm)
    held = (gate_v, up_v)

    def copy(w, i):
        cols = pl.ds(pl.multiple_of(i * CHUNK, CHUNK), CHUNK)
        return pltpu.make_async_copy(hbm[w].at[:, cols], held[w].at[:, cols], sems.at[w, i])

    for i in range(chunks):
        for w in range(2):
            copy(w, i).start()
    low = TILE * R - 1
    local = lax.broadcasted_iota(jnp.int32, (TILE, R), 0) * R + lax.broadcasted_iota(
        jnp.int32, (TILE, R), 1
    )
    seeds = [seed_ref[0], seed_ref[1]]
    tables = [first_mix(local, low, seed) for seed in seeds]
    acc[...] = jnp.zeros_like(acc)

    def step(i, fill, use):
        if use is not None:
            for w in range(2):
                copy(w, i - 1).wait()
        for w in range(2):
            part = None
            for t in range(CHUNK // TILE):
                if fill is not None:
                    start = base_mix((i * CHUNK + t * TILE) * R, low, seeds[w])
                    fill[w, t * TILE : (t + 1) * TILE, :] = finish(tables[w] + start)
                if use is not None and (t + 1) * TILE % PIECE == 0:
                    d = (t + 1) * TILE - PIECE
                    cols = pl.ds(pl.multiple_of((i - 1) * CHUNK + d, PIECE), PIECE)
                    product = jnp.dot(
                        held[w][:, cols], use[w, d : d + PIECE, :], preferred_element_type=F32
                    )
                    part = product if part is None else part + product
            if part is not None:
                acc[w] += part

    step(0, even, None)

    def body(k, carry):
        step(2 * k + 1, odd, even)
        step(2 * k + 2, even, odd)
        return carry

    lax.fori_loop(0, chunks // 2 - 1, body, 0)
    step(chunks - 1, odd, even)
    step(chunks, None, odd)
    for w in range(2):
        out_ref[w] = acc[w].astype(BF16).astype(F32).T


def reduce_both(seeds, gate_cot, up_cot):
    rows = gate_cot.shape[0]
    return pl.pallas_call(
        reduce_kernel,
        in_specs=[
            pl.BlockSpec(memory_space=pltpu.SMEM),
            pl.BlockSpec(memory_space=pltpu.HBM),
            pl.BlockSpec(memory_space=pltpu.HBM),
        ],
        out_specs=pl.BlockSpec(memory_space=pltpu.VMEM),
        out_shape=jax.ShapeDtypeStruct((2, R, rows), F32),
        scratch_shapes=[
            pltpu.VMEM((rows, FF), BF16),
            pltpu.VMEM((rows, FF), BF16),
            pltpu.VMEM((2, CHUNK, R), BF16),
            pltpu.VMEM((2, CHUNK, R), BF16),
            pltpu.VMEM((2, rows, R), F32),
            pltpu.SemaphoreType.DMA((2, FF // CHUNK)),
        ],
        compiler_params=pltpu.CompilerParams(vmem_limit_bytes=50 * 2**20),
        cost_estimate=pl.CostEstimate(
            flops=4 * rows * FF * R, bytes_accessed=4 * rows * FF, transcendentals=0
        ),
        name="reduce_both",
    )(seeds, gate_cot, up_cot)


def place():
    return tuple(lax.axis_index(name).astype(jnp.int32) for name in AXES)


def pooled_columns(core, x, y, k, zl, j):
    zero = core == 0
    at = lax.rem(jnp.where(zero, x, y) + k, 4)
    a = zl * 4096 + j * jnp.where(zero, 1024, 128) + at * jnp.where(zero, 128, 1024)
    return pl.ds(pl.multiple_of(a + core * 512, 128), 128)


def theirs_kernel(act_ref, *outs):
    x, _, core, _, y = place()
    for k, out in enumerate(outs):
        for n in range(8):
            cols = pooled_columns(1 - core, x, y, k, n // 4, n % 4)
            out[:, n * 128 : (n + 1) * 128] = act_ref[:, cols].astype(F32)


def pairs_kernel(act_ref, *rest):
    x, _, core, _, y = place()
    for k, (far, out) in enumerate(zip(rest[:3], rest[3:])):
        rows = act_ref.shape[0]
        for n in range(8):
            cols = pooled_columns(core, x, y, k + 1, n // 4, n % 4)
            out[:rows, n * 128 : (n + 1) * 128] = act_ref[:, cols].astype(F32)
        out[rows:, :] = far[...]


def rows_for(kernel, name, height, count, act, *far):
    return pl.pallas_call(
        kernel,
        in_specs=[pl.BlockSpec(memory_space=pltpu.VMEM)] * (1 + len(far)),
        out_specs=[pl.BlockSpec(memory_space=pltpu.VMEM)] * count,
        out_shape=[jax.ShapeDtypeStruct((height, 1024), F32)] * count,
        compiler_params=pltpu.CompilerParams(vmem_limit_bytes=10 * 2**20),
        cost_estimate=pl.CostEstimate(
            flops=height * 8192, bytes_accessed=6 * 2**20, transcendentals=0
        ),
        name=name,
    )(act, *far)


def grad_kernel(act_ref, *rest):
    x, _, core, _, y = place()
    second_at = jnp.where(core == 0, y, x)
    others = rest[:4]
    reds = rest[4:8]
    outs = rest[8:12]
    left = jnp.concatenate(
        [
            jnp.concatenate(
                [red[side, w].astype(BF16) for red in reds for side in range(2)], axis=1
            )
            for w in range(2)
        ],
        axis=0,
    )
    for k in range(4):
        j = lax.rem(second_at + k, 4)
        columns = []
        for zl in range(2):
            b = zl * 512 + j * 128
            columns.append(
                jnp.concatenate(
                    [act_ref[:, pooled_columns(core, x, y, 0, zl, j)]]
                    + [
                        other[:, pl.ds(pl.multiple_of(b, 128), 128)].astype(BF16)
                        for other in others
                    ],
                    axis=0,
                )
            )
        product = jnp.dot(
            left, jnp.concatenate(columns, axis=1), preferred_element_type=F32
        )
        for zl in range(2):
            for w in range(2):
                outs[k][w, zl] = product[
                    w * 128 : (w + 1) * 128, zl * 128 : (zl + 1) * 128
                ]


def partial_grads(act, others, reds):
    return pl.pallas_call(
        grad_kernel,
        in_specs=[pl.BlockSpec(memory_space=pltpu.VMEM)] * 9,
        out_specs=[pl.BlockSpec(memory_space=pltpu.VMEM)] * 4,
        out_shape=[jax.ShapeDtypeStruct((2, 2, 128, 128), F32)] * 4,
        compiler_params=pltpu.CompilerParams(vmem_limit_bytes=16 * 2**20),
        cost_estimate=pl.CostEstimate(
            flops=2 * 256 * 1024 * 1024, bytes_accessed=6 * 2**20, transcendentals=0
        ),
        name="partial_grads",
    )(act, *others, *reds)


def columns_kernel(seed_ref, out_ref):
    x, zh, core, _, _ = place()
    low = 128 * R - 1
    local = lax.broadcasted_iota(jnp.int32, (R, 128), 1) * R + lax.broadcasted_iota(
        jnp.int32, (R, 128), 0
    )
    count = out_ref.shape[2]
    base = ((x * 2 + zh) * 2 + core) * count
    for w in range(2):
        seed = seed_ref[w]
        table = first_mix(local, low, seed)
        for t in range(count // 128):
            start = base_mix((base + t * 128) * R, low, seed)
            out_ref[w, :, t * 128 : (t + 1) * 128] = finish(table + start)


def basis_columns(seeds, count):
    return pl.pallas_call(
        columns_kernel,
        in_specs=[pl.BlockSpec(memory_space=pltpu.SMEM)],
        out_specs=pl.BlockSpec(memory_space=pltpu.VMEM),
        out_shape=jax.ShapeDtypeStruct((2, R, count), BF16),
        compiler_params=pltpu.CompilerParams(vmem_limit_bytes=4 * 2**20),
        cost_estimate=pl.CostEstimate(
            flops=40 * R * count, bytes_accessed=4 * R * count, transcendentals=0
        ),
        name="basis_columns",
    )(seeds)


def update_kernel(
    basis_ref, gf_ref, gs_ref, uf_ref, us_ref, *rest
):
    grads = rest[:8]
    step_out = rest[8:10]
    moment_out = rest[10:14]
    step_v = rest[14:16]
    moment_v = rest[16:20]
    sems = rest[20]
    firsts = (gf_ref, uf_ref)
    seconds = (gs_ref, us_ref)
    pending = []
    x, _, core, _, _ = place()
    for i in range(8):
        side = core if i < 4 else 1 - core
        start = (side * 4 + lax.rem(x - i % 4 + 4, 4)) * 128
        rows = pl.ds(pl.multiple_of(start, 128), 128)
        for w in range(2):
            grad = grads[i][w].T * (1.0 / TOKENS)
            first_new = beta_one * firsts[w][rows, :] + (1.0 - beta_one) * grad
            second_new = beta_two * seconds[w][rows, :] + (1.0 - beta_two) * grad * grad
            moment_v[2 * w][rows, :] = first_new
            moment_v[2 * w + 1][rows, :] = second_new
            direction = (
                first_new / bias_one / (jnp.sqrt(second_new / bias_two) + epsilon)
            ).astype(BF16)
            step_v[w][rows, :] = jnp.dot(
                direction, basis_ref[w], preferred_element_type=F32
            ).astype(BF16)
            n = 0
            for src, dst in (
                (step_v[w], step_out[w]),
                (moment_v[2 * w], moment_out[2 * w]),
                (moment_v[2 * w + 1], moment_out[2 * w + 1]),
            ):
                copy = pltpu.make_async_copy(src.at[rows, :], dst.at[rows, :], sems.at[i, w, n])
                copy.start()
                pending.append(copy)
                n += 1
    for copy in pending:
        copy.wait()


def update(basis, moments, grads):
    rows, cols = moments[0].shape[0], basis.shape[2]
    return pl.pallas_call(
        update_kernel,
        in_specs=[pl.BlockSpec(memory_space=pltpu.VMEM)] * 13,
        out_specs=[pl.BlockSpec(memory_space=pl.ANY)] * 6,
        out_shape=[jax.ShapeDtypeStruct((rows, cols), BF16)] * 2
        + [jax.ShapeDtypeStruct((rows, R), F32)] * 4,
        scratch_shapes=[pltpu.VMEM((rows, cols), BF16)] * 2
        + [pltpu.VMEM((rows, R), F32)] * 4
        + [pltpu.SemaphoreType.DMA((8, 2, 3))],
        compiler_params=pltpu.CompilerParams(vmem_limit_bytes=16 * 2**20),
        cost_estimate=pl.CostEstimate(
            flops=4 * rows * cols * R, bytes_accessed=12 * 2**20, transcendentals=0
        ),
        name="update",
    )(basis, *moments, *grads)


def send(value, to):
    perm = []
    for source in range(128):
        x, zh, core, zl, y = (int(v) for v in np.unravel_index(source, SIZES))
        nx, nz, ncore, ny = to(x, zh * 2 + zl, core, y)
        nz %= 4
        target = int(
            np.ravel_multi_index((nx % 4, nz // 2, ncore, nz % 2, ny % 4), SIZES)
        )
        perm.append((source, target))
    return lax.ppermute(value, AXES, perm)


def swap_core(value):
    return lax.ppermute(value, "core", [(0, 1), (1, 0)])


def local(act, gate_cot, up_cot, seeds, gate_first, gate_second, up_first, up_second):
    zl = lax.axis_index("zl")

    def pool(value, k):
        return send(value, lambda x, z, c, y: (x + k, z, c, y) if c == 0 else (x, z, c, y + k))

    def across(value, k):
        return send(value, lambda x, z, c, y: (x, z, c, y + k) if c == 0 else (x + k, z, c, y))

    rows = act.shape[0]
    swapped = [swap_core(v) for v in rows_for(theirs_kernel, "theirs", rows, 4, act)]
    pairs = rows_for(pairs_kernel, "pairs", 2 * rows, 3, act, *swapped[1:])
    moved = [pool(pairs[k - 1], k) for k in range(1, 4)]

    basis = basis_columns(seeds, FF // 16)

    late_seeds, pairs = lax.optimization_barrier((seeds, pairs))
    reduced = reduce_both(late_seeds, gate_cot, up_cot)
    pair = jnp.stack([reduced, swap_core(reduced)])
    pooled = [pool(pair, k) for k in (1, 2)]
    last, moved = lax.optimization_barrier((pair, moved))
    pooled.append(pool(last, 3))

    parts = partial_grads(act, [swapped[0]] + moved, [pair] + pooled)

    mine, basis = lax.optimization_barrier((parts[0], basis))
    for k in range(1, 4):
        mine = mine + across(parts[k], k)

    away = lax.dynamic_index_in_dim(mine, 1 - zl, 1, keepdims=False)
    here = lax.dynamic_index_in_dim(mine, zl, 1, keepdims=False)
    done = here + send(away, lambda x, z, c, y: (x, z + 1, c, y))
    done = done + send(away, lambda x, z, c, y: (x, z - 1, c, y))
    done = done + send(here, lambda x, z, c, y: (x, z + 2, c, y))

    own = [done] + [
        send(done, lambda x, z, c, y, k=k: (x + k, z, c, y)) for k in range(1, 4)
    ]
    theirs = [swap_core(piece) for piece in own]
    gate_step, up_step, gfn, gsn, ufn, usn = update(
        basis,
        (gate_first, gate_second, up_first, up_second),
        own + theirs,
    )
    return gate_step, up_step, gfn, gsn, ufn, usn


def solution(mesh):
    fine = Mesh(mesh.devices.reshape(SIZES), AXES)
    both = ("x", "zh", "core", "zl", "y")
    dp = ("x", "zh", "core")
    fsdp = ("zl", "y")
    return jax.shard_map(
        local,
        mesh=fine,
        in_specs=(P(both, None),) * 3 + (P(),) + (P(fsdp, None),) * 4,
        out_specs=(P(fsdp, dp),) * 2 + (P(fsdp, None),) * 4,
        check_vma=False,
    )
```

time: 311 us -> 85.4 us (0.27)
  waiting for transfers between devices: 209 us -> 20.1 us
  matrix products: 46.7 us -> 0 us
  starting transfers between devices: 0.08 us -> 37.2 us
  Pallas kernels: 0 us -> 24.3 us
  other arithmetic: 24.7 us -> 1.14 us
  local copies, waits for them, and re-layouts: 16 us -> 1.65 us
  between operations: 14.1 us -> 0.92 us
    psum x1 -> x0, waiting for transfers between devices: 113 us -> none  [local(): whole = lax.psum(whole, 'dp')]
    reduce_scatter x1 -> x0, waiting for transfers between devices: 96.1 us -> none  [local(): summed = lax.psum_scatter(whole, 'fsdp', scatter_dimension=0, tiled=True)]
    dot_general x5 -> x0, matrix products: 46.7 us -> none  [the longest x1 17.2 us: local(): jnp.dot(gate_cotangent, gate_basis, preferred_element_type=jnp.float32)]
    ppermute x0 -> x24, starting transfers between devices: none -> 37.2 us  [the longest x15 22.5 us: send(): return lax.ppermute(value, AXES, perm)]
    convert_element_type x2 -> x0, other arithmetic: 24.7 us -> none  [the longest x1 22.4 us: projection(): return (unit * math.sqrt(3.0 / rank)).astype(jnp.bfloat16)]
    pallas_call x0 -> x6, Pallas kernels: none -> 24.3 us  [the longest x1 17.1 us: reduce_both(): pl.pallas_call(reduce_kernel, in_specs=[pl.BlockSpec(memory_space=pltpu.S...]
    ppermute x0 -> x24, waiting for transfers between devices: none -> 20.1 us  [the longest x15 15.3 us: send(): return lax.ppermute(value, AXES, perm)]
    unnamed x14, local copies, waits for them, and re-layouts: 13.4 us -> 1.62 us
  transfers between devices with their start and end apart: 2 -> 24, of which waited for: 2 -> 12; matrix products, arithmetic and copies ran while one was open for 9% -> 0% of each run, Pallas kernels for 0% -> 22%
where the time goes in v1:
time: 85.4 us; the launch traced here: 85.2 us
  starting transfers between devices  37.2 us (44%)
  Pallas kernels  24.3 us (28%)
  waiting for transfers between devices  20.1 us (24%)
  local copies, waits for them, and re-layouts  1.65 us (2%)
  other arithmetic  1.14 us (1%)
  between operations  0.92 us (1%)
    ppermute x15, starting transfers between devices, send(): return lax.ppermute(value, AXES, perm)  22.5 us
    pallas_call x1, Pallas kernels, reduce_both(): pl.pallas_call(reduce_kernel, in_specs=[pl.BlockSpec(memory_space=pltpu.S...  17.1 us
    ppermute x15, waiting for transfers between devices, send(): return lax.ppermute(value, AXES, perm)  15.3 us
    ppermute x9, starting transfers between devices, swap_core(): return lax.ppermute(value, 'core', [(0, 1), (1, 0)])  14.7 us
    ppermute x9, waiting for transfers between devices, swap_core(): return lax.ppermute(value, 'core', [(0, 1), (1, 0)])  4.77 us
    pallas_call x1, Pallas kernels, update(): pl.pallas_call(update_kernel, in_specs=[pl.BlockSpec(memory_space=pltpu.V...  4.4 us
  transfers between devices with their start and end apart: 24, of which 12 were waited for; matrix products, arithmetic and copies ran while one was open for 0% of the time, Pallas kernels for 22%

profile of v1, /device:TPU:1, one launch (start us, length us, event | category | flops | bytes accessed | tf_op | source)
XLA Modules:
  0.0 85.2 jit_solution(14767627973562146797)
XLA Ops:
  0.6 1.6 %copy-done = bf16[128,8192]{1,0:T(8,128)(2,1)S(1)} copy-done((bf16[128,8192]{1,0:T(8,128)(2,1)S(1)}, bf16[128,8192]{1,0:T(8,128)(2,1)}, u32[]{:S(2)}) %copy-start) | copy-done | bytes 2097176
  2.5 1.5 %collective-permute-start.1 = (f32[128,1024]{1,0:T(8,128)S(1)}, f32[128,1024]{1,0:T(8,128)S(1)}, u32[]{:S(2)}, u32[]{:S(2)}) collective-permute-start(f32[128,1024]{1,0:T(8,128)S(1)} %get-tuple-element.25), channel_id=1, source_target_pairs={{0,8},{8,0},{1,9},{9,1},{2,10},{10,2},{3,11},{11,3},{4,12},{12,4},... | collective-permute-start | bytes 1572872 | tf_op jit(solution)/shard_map/ppermute | solution.py:342
  7.4 1.4 %collective-permute-start.5 = (f32[256,1024]{1,0:T(8,128)S(1)}, f32[256,1024]{1,0:T(8,128)S(1)}, u32[]{:S(2)}, u32[]{:S(2)}) collective-permute-start(f32[256,1024]{1,0:T(8,128)S(1)} %get-tuple-element.28), channel_id=1, source_target_pairs={{0,32},{1,33},{2,34},{3,35},{4,36},{5,37},{6,38},{7,39},{8,9},{9,1... | collective-permute-start | bytes 3145736 | tf_op jit(solution)/shard_map/ppermute | solution.py:338
  8.8 2.6 %collective-permute-start.6 = (f32[256,1024]{1,0:T(8,128)S(1)}, f32[256,1024]{1,0:T(8,128)S(1)}, u32[]{:S(2)}, u32[]{:S(2)}) collective-permute-start(f32[256,1024]{1,0:T(8,128)S(1)} %get-tuple-element.29), channel_id=1, source_target_pairs={{0,64},{1,65},{2,66},{3,67},{4,68},{5,69},{6,70},{7,71},{8,10},{9,... | collective-permute-start | bytes 3145736 | tf_op jit(solution)/shard_map/ppermute | solution.py:338
  11.4 1.1 %collective-permute-start.7 = (f32[256,1024]{1,0:T(8,128)S(1)}, f32[256,1024]{1,0:T(8,128)S(1)}, u32[]{:S(2)}, u32[]{:S(2)}) collective-permute-start(f32[256,1024]{1,0:T(8,128)S(1)} %get-tuple-element.30), channel_id=1, source_target_pairs={{0,96},{1,97},{2,98},{3,99},{4,100},{5,101},{6,102},{7,103},{8,11}... | collective-permute-start | bytes 3145736 | tf_op jit(solution)/shard_map/ppermute | solution.py:338
  13.6 17.1 %reduce_both.1 = f32[2,128,128]{2,1,0:T(8,128)S(1)} custom-call(s32[2]{0:T(128)S(1)} %copy-done.6, bf16[128,28672]{1,0:T(8,128)(2,1)} %gate_hbm.1, bf16[128,28672]{1,0:T(8,128)(2,1)} %up_hbm.1), custom_call_target="tpu_custom_call" | custom-call | flops 1879048192 | bytes 14680064 | tf_op jit(solution)/shard_map/reduce_both/pallas_call | solution.py:114
  30.9 1.3 %collective-permute-done.4 = f32[2,128,128]{2,1,0:T(8,128)S(1)} collective-permute-done((f32[2,128,128]{2,1,0:T(8,128)S(1)}, f32[2,128,128]{2,1,0:T(8,128)S(1)}, u32[]{:S(2)}, u32[]{:S(2)}) %collective-permute-start.4) | collective-permute-done | bytes 131104 | tf_op jit(solution)/shard_map/ppermute | solution.py:342
  32.2 3.0 %collective-permute-start.9 = (f32[2,2,128,128]{3,2,1,0:T(8,128)S(1)}, f32[2,2,128,128]{3,2,1,0:T(8,128)S(1)}, u32[]{:S(2)}, u32[]{:S(2)}) collective-permute-start(f32[2,2,128,128]{3,2,1,0:T(8,128)S(1)} %pad_maximum_fusion.rest_4_), channel_id=1, source_target_pairs={{0,64},{1,65},{2,66},{3,67},{4,68},{5,69},{6,70},{7,71},{8,10},{9,... | collective-permute-start | bytes 786440 | tf_op jit(solution)/shard_map/ppermute | solution.py:338
  35.6 2.3 %collective-permute-start.10 = (f32[2,2,128,128]{3,2,1,0:T(8,128)S(1)}, f32[2,2,128,128]{3,2,1,0:T(8,128)S(1)}, u32[]{:S(2)}, u32[]{:S(2)}) collective-permute-start(f32[2,2,128,128]{3,2,1,0:T(8,128)S(1)} %pad_maximum_fusion.rest_4_), channel_id=1, source_target_pairs={{0,96},{1,97},{2,98},{3,99},{4,100},{5,101},{6,102},{7,103},{8,11}... | collective-permute-start | bytes 786440 | tf_op jit(solution)/shard_map/ppermute | solution.py:338
  37.9 1.4 %collective-permute-done.9.rest_6_ = f32[2,2,128,128]{3,2,1,0:T(8,128)S(1)} collective-permute-done((f32[2,2,128,128]{3,2,1,0:T(8,128)S(1)}, f32[2,2,128,128]{3,2,1,0:T(8,128)S(1)}, u32[]{:S(2)}, u32[]{:S(2)}) %collective-permute-start.9) | collective-permute-done | bytes 262176 | tf_op jit(solution)/shard_map/ppermute | solution.py:338
  39.3 2.8 %collective-permute-done.8.rest_5_ = f32[2,2,128,128]{3,2,1,0:T(8,128)S(1)} collective-permute-done((f32[2,2,128,128]{3,2,1,0:T(8,128)S(1)}, f32[2,2,128,128]{3,2,1,0:T(8,128)S(1)}, u32[]{:S(2)}, u32[]{:S(2)}) %collective-permute-start.8) | collective-permute-done | bytes 262176 | tf_op jit(solution)/shard_map/ppermute | solution.py:338
  43.7 2.1 %collective-permute-start.12 = (f32[2,2,128,128]{3,2,1,0:T(8,128)S(1)}, f32[2,2,128,128]{3,2,1,0:T(8,128)}, u32[]{:S(2)}, u32[]{:S(2)}) collective-permute-start(f32[2,2,128,128]{3,2,1,0:T(8,128)S(1)} %get-tuple-element.40), channel_id=1, source_target_pairs={{0,2},{1,3},{2,0},{3,1},{4,6},{5,7},{6,4},{7,5},{8,72},{9,73},{10,... | collective-permute-start | bytes 786440 | tf_op jit(solution)/shard_map/ppermute | solution.py:338
  46.7 1.2 %basis_columns.1.basis_ref = bf16[2,128,1792]{2,1,0:T(8,128)(2,1)S(1)} custom-call(s32[2]{0:T(128)S(1)} %copy-done.6), custom_call_target="tpu_custom_call" | custom-call | flops 9175040 | bytes 917504 | tf_op jit(solution)/shard_map/basis_columns/pallas_call | solution.py:253
  48.0 5.1 %collective-permute-done.11 = f32[2,2,128,128]{3,2,1,0:T(8,128)S(1)} collective-permute-done((f32[2,2,128,128]{3,2,1,0:T(8,128)S(1)}, f32[2,2,128,128]{3,2,1,0:T(8,128)S(1)}, u32[]{:S(2)}, u32[]{:S(2)}) %collective-permute-start.11) | collective-permute-done | bytes 262176 | tf_op jit(solution)/shard_map/ppermute | solution.py:338
  53.7 1.1 %add_add_fusion = f32[2,2,128,128]{3,2,1,0:T(8,128)S(1)} fusion(f32[2,2,128,128]{3,2,1,0:T(8,128)} %collective-permute-done.13, f32[2,2,128,128]{3,2,1,0:T(8,128)} %collective-permute-done.12, f32[2,2,128,128]{3,2,1,0:T(8,128)S(1)} %get-tuple-element.38, f32[2,2,128,128]{3,2,1,0:T(8,128)S(1)} %collective-permute-done.11), kind=kLoop, calls=%fused_computation.1 | loop fusion | flops 196608 | bytes 1310720 | tf_op jit(solution)/shard_map/add | solution.py:372
  54.8 3.8 %collective-permute-start.15 = (f32[2,128,128]{2,1,0:T(8,128)S(1)}, f32[2,128,128]{2,1,0:T(8,128)S(1)}, u32[]{:S(2)}, u32[]{:S(2)}) collective-permute-start(f32[2,128,128]{2,1,0:T(8,128)S(1)} %get-tuple-element.42), channel_id=1, source_target_pairs={{0,20},{1,21},{2,22},{3,23},{4,0},{5,1},{6,2},{7,3},{8,28},{9,29},... | collective-permute-start | bytes 393224 | tf_op jit(solution)/shard_map/ppermute | solution.py:338
  58.7 1.4 %collective-permute-start.16 = (f32[2,128,128]{2,1,0:T(8,128)S(1)}, f32[2,128,128]{2,1,0:T(8,128)S(1)}, u32[]{:S(2)}, u32[]{:S(2)}) collective-permute-start(f32[2,128,128]{2,1,0:T(8,128)S(1)} %get-tuple-element.43), channel_id=1, source_target_pairs={{0,16},{1,17},{2,18},{3,19},{4,20},{5,21},{6,22},{7,23},{8,24},{9,... | collective-permute-start | bytes 393224 | tf_op jit(solution)/shard_map/ppermute | solution.py:338
  60.6 4.5 %collective-permute-done.14 = f32[2,128,128]{2,1,0:T(8,128)S(1)} collective-permute-done((f32[2,128,128]{2,1,0:T(8,128)S(1)}, f32[2,128,128]{2,1,0:T(8,128)S(1)}, u32[]{:S(2)}, u32[]{:S(2)}) %collective-permute-start.14) | collective-permute-done | bytes 131104 | tf_op jit(solution)/shard_map/ppermute | solution.py:338
  65.1 2.4 %collective-permute-start.19 = (f32[2,128,128]{2,1,0:T(8,128)S(1)}, f32[2,128,128]{2,1,0:T(8,128)S(1)}, u32[]{:S(2)}, u32[]{:S(2)}) collective-permute-start(f32[2,128,128]{2,1,0:T(8,128)S(1)} %add_add_fusion.1.rest_0_), channel_id=1, source_target_pairs={{0,96},{1,97},{2,98},{3,99},{4,100},{5,101},{6,102},{7,103},{8,104... | collective-permute-start | bytes 393224 | tf_op jit(solution)/shard_map/ppermute | solution.py:338
  68.2 4.6 %collective-permute-start.20 = (f32[2,128,128]{2,1,0:T(8,128)S(1)}, f32[2,128,128]{2,1,0:T(8,128)S(1)}, u32[]{:S(2)}, u32[]{:S(2)}) collective-permute-start(f32[2,128,128]{2,1,0:T(8,128)S(1)} %add_add_fusion.1.rest_0_), channel_id=1, source_target_pairs={{0,8},{8,0},{1,9},{9,1},{2,10},{10,2},{3,11},{11,3},{4,12},{12,4},... | collective-permute-start | bytes 393224 | tf_op jit(solution)/shard_map/ppermute | solution.py:342
  72.9 3.0 %collective-permute-start.23 = (f32[2,128,128]{2,1,0:T(8,128)S(1)}, f32[2,128,128]{2,1,0:T(8,128)S(1)}, u32[]{:S(2)}, u32[]{:S(2)}) collective-permute-start(f32[2,128,128]{2,1,0:T(8,128)S(1)} %collective-permute-done.19.rest_3_), channel_id=1, source_target_pairs={{0,8},{8,0},{1,9},{9,1},{2,10},{10,2},{3,11},{11,3},{4,12},{12,4},... | collective-permute-start | bytes 393224 | tf_op jit(solution)/shard_map/ppermute | solution.py:342
  75.8 2.7 %collective-permute-start.22 = (f32[2,128,128]{2,1,0:T(8,128)S(1)}, f32[2,128,128]{2,1,0:T(8,128)S(1)}, u32[]{:S(2)}, u32[]{:S(2)}) collective-permute-start(f32[2,128,128]{2,1,0:T(8,128)S(1)} %collective-permute-done.18.rest_2_), channel_id=1, source_target_pairs={{0,8},{8,0},{1,9},{9,1},{2,10},{10,2},{3,11},{11,3},{4,12},{12,4},... | collective-permute-start | bytes 393224 | tf_op jit(solution)/shard_map/ppermute | solution.py:342
  78.5 1.2 %collective-permute-start.21 = (f32[2,128,128]{2,1,0:T(8,128)S(1)}, f32[2,128,128]{2,1,0:T(8,128)S(1)}, u32[]{:S(2)}, u32[]{:S(2)}) collective-permute-start(f32[2,128,128]{2,1,0:T(8,128)S(1)} %collective-permute-done.17.rest_1_), channel_id=1, source_target_pairs={{0,8},{8,0},{1,9},{9,1},{2,10},{10,2},{3,11},{11,3},{4,12},{12,4},... | collective-permute-start | bytes 393224 | tf_op jit(solution)/shard_map/ppermute | solution.py:342
  80.7 4.4 %update.1 = (bf16[1024,1792]{1,0:T(8,128)(2,1)}, bf16[1024,1792]{1,0:T(8,128)(2,1)}, f32[1024,128]{1,0:T(8,128)}, f32[1024,128]{1,0:T(8,128)}, f32[1024,128]{1,0:T(8,128)}, /*index=5*/f32[1024,128]{1,0:T(8,128)}) custom-call(bf16[2,128,1792]{2,1,0:T(8,128)(2,1)S(1)} %basis_columns.1.basis_ref, f32[1024,128]{1,0:T(8,128)S(1)} %copy-done.2, ...), custom_call_target="tpu_custom_call" | custom-call | flops 939524096 | bytes 12582912 | tf_op jit(solution)/shard_map/update/pallas_call | solution.py:311
  (48 shorter events, 10.6 us)
Async XLA Ops:
  2.5 3.0 %collective-permute-start.1 = (f32[128,1024]{1,0:T(8,128)S(1)}, f32[128,1024]{1,0:T(8,128)S(1)}, u32[]{:S(2)}, u32[]{:S(2)}) collective-permute-start(f32[128,1024]{1,0:T(8,128)S(1)} %get-tuple-element.25), channel_id=1, source_target_pairs={{0,8},{8,0},{1,9},{9,1},{2,10},{10,2},{3,11},{11,3},{4,12},{12,4},... | collective-permute-start | bytes 1572872 | tf_op jit(solution)/shard_map/ppermute | solution.py:342
  4.0 2.3 %collective-permute-start.2 = (f32[128,1024]{1,0:T(8,128)S(1)}, f32[128,1024]{1,0:T(8,128)S(1)}, u32[]{:S(2)}, u32[]{:S(2)}) collective-permute-start(f32[128,1024]{1,0:T(8,128)S(1)} %get-tuple-element.26), channel_id=1, source_target_pairs={{0,8},{8,0},{1,9},{9,1},{2,10},{10,2},{3,11},{11,3},{4,12},{12,4},... | collective-permute-start | bytes 1572872 | tf_op jit(solution)/shard_map/ppermute | solution.py:342
  4.1 2.9 %collective-permute-start.3 = (f32[128,1024]{1,0:T(8,128)S(1)}, f32[128,1024]{1,0:T(8,128)S(1)}, u32[]{:S(2)}, u32[]{:S(2)}) collective-permute-start(f32[128,1024]{1,0:T(8,128)S(1)} %get-tuple-element.27), channel_id=1, source_target_pairs={{0,8},{8,0},{1,9},{9,1},{2,10},{10,2},{3,11},{11,3},{4,12},{12,4},... | collective-permute-start | bytes 1572872 | tf_op jit(solution)/shard_map/ppermute | solution.py:342
  7.4 27.8 %collective-permute-start.5 = (f32[256,1024]{1,0:T(8,128)S(1)}, f32[256,1024]{1,0:T(8,128)S(1)}, u32[]{:S(2)}, u32[]{:S(2)}) collective-permute-start(f32[256,1024]{1,0:T(8,128)S(1)} %get-tuple-element.28), channel_id=1, source_target_pairs={{0,32},{1,33},{2,34},{3,35},{4,36},{5,37},{6,38},{7,39},{8,9},{9,1... | collective-permute-start | bytes 3145736 | tf_op jit(solution)/shard_map/ppermute | solution.py:338
  8.8 26.8 %collective-permute-start.6 = (f32[256,1024]{1,0:T(8,128)S(1)}, f32[256,1024]{1,0:T(8,128)S(1)}, u32[]{:S(2)}, u32[]{:S(2)}) collective-permute-start(f32[256,1024]{1,0:T(8,128)S(1)} %get-tuple-element.29), channel_id=1, source_target_pairs={{0,64},{1,65},{2,66},{3,67},{4,68},{5,69},{6,70},{7,71},{8,10},{9,... | collective-permute-start | bytes 3145736 | tf_op jit(solution)/shard_map/ppermute | solution.py:338
  11.4 24.2 %collective-permute-start.7 = (f32[256,1024]{1,0:T(8,128)S(1)}, f32[256,1024]{1,0:T(8,128)S(1)}, u32[]{:S(2)}, u32[]{:S(2)}) collective-permute-start(f32[256,1024]{1,0:T(8,128)S(1)} %get-tuple-element.30), channel_id=1, source_target_pairs={{0,96},{1,97},{2,98},{3,99},{4,100},{5,101},{6,102},{7,103},{8,11}... | collective-permute-start | bytes 3145736 | tf_op jit(solution)/shard_map/ppermute | solution.py:338
  12.5 25.4 %collective-permute-start = (f32[128,1024]{1,0:T(8,128)S(1)}, f32[128,1024]{1,0:T(8,128)S(1)}, u32[]{:S(2)}, u32[]{:S(2)}) collective-permute-start(f32[128,1024]{1,0:T(8,128)S(1)} %get-tuple-element.24), channel_id=1, source_target_pairs={{0,8},{8,0},{1,9},{9,1},{2,10},{10,2},{3,11},{11,3},{4,12},{12,4},... | collective-permute-start | bytes 1572872 | tf_op jit(solution)/shard_map/ppermute | solution.py:342
  30.7 1.4 %collective-permute-start.4 = (f32[2,128,128]{2,1,0:T(8,128)S(1)}, f32[2,128,128]{2,1,0:T(8,128)S(1)}, u32[]{:S(2)}, u32[]{:S(2)}) collective-permute-start(f32[2,128,128]{2,1,0:T(8,128)S(1)} %reduce_both.1), channel_id=1, source_target_pairs={{0,8},{8,0},{1,9},{9,1},{2,10},{10,2},{3,11},{11,3},{4,12},{12,4},... | collective-permute-start | bytes 393224 | tf_op jit(solution)/shard_map/ppermute | solution.py:342
  32.2 7.1 %collective-permute-start.9 = (f32[2,2,128,128]{3,2,1,0:T(8,128)S(1)}, f32[2,2,128,128]{3,2,1,0:T(8,128)S(1)}, u32[]{:S(2)}, u32[]{:S(2)}) collective-permute-start(f32[2,2,128,128]{3,2,1,0:T(8,128)S(1)} %pad_maximum_fusion.rest_4_), channel_id=1, source_target_pairs={{0,64},{1,65},{2,66},{3,67},{4,68},{5,69},{6,70},{7,71},{8,10},{9,... | collective-permute-start | bytes 786440 | tf_op jit(solution)/shard_map/ppermute | solution.py:338
  35.2 6.9 %collective-permute-start.8 = (f32[2,2,128,128]{3,2,1,0:T(8,128)S(1)}, f32[2,2,128,128]{3,2,1,0:T(8,128)S(1)}, u32[]{:S(2)}, u32[]{:S(2)}) collective-permute-start(f32[2,2,128,128]{3,2,1,0:T(8,128)S(1)} %pad_maximum_fusion.rest_4_), channel_id=1, source_target_pairs={{0,32},{1,33},{2,34},{3,35},{4,36},{5,37},{6,38},{7,39},{8,9},{9,1... | collective-permute-start | bytes 786440 | tf_op jit(solution)/shard_map/ppermute | solution.py:338
  35.6 6.8 %collective-permute-start.10 = (f32[2,2,128,128]{3,2,1,0:T(8,128)S(1)}, f32[2,2,128,128]{3,2,1,0:T(8,128)S(1)}, u32[]{:S(2)}, u32[]{:S(2)}) collective-permute-start(f32[2,2,128,128]{3,2,1,0:T(8,128)S(1)} %pad_maximum_fusion.rest_4_), channel_id=1, source_target_pairs={{0,96},{1,97},{2,98},{3,99},{4,100},{5,101},{6,102},{7,103},{8,11}... | collective-permute-start | bytes 786440 | tf_op jit(solution)/shard_map/ppermute | solution.py:338
  43.4 9.7 %collective-permute-start.11 = (f32[2,2,128,128]{3,2,1,0:T(8,128)S(1)}, f32[2,2,128,128]{3,2,1,0:T(8,128)S(1)}, u32[]{:S(2)}, u32[]{:S(2)}) collective-permute-start(f32[2,2,128,128]{3,2,1,0:T(8,128)S(1)} %get-tuple-element.39), channel_id=1, source_target_pairs={{0,1},{1,2},{2,3},{3,0},{4,5},{5,6},{6,7},{7,4},{8,40},{9,41},{10,... | collective-permute-start | bytes 786440 | tf_op jit(solution)/shard_map/ppermute | solution.py:338
  43.7 9.3 %collective-permute-start.12 = (f32[2,2,128,128]{3,2,1,0:T(8,128)S(1)}, f32[2,2,128,128]{3,2,1,0:T(8,128)}, u32[]{:S(2)}, u32[]{:S(2)}) collective-permute-start(f32[2,2,128,128]{3,2,1,0:T(8,128)S(1)} %get-tuple-element.40), channel_id=1, source_target_pairs={{0,2},{1,3},{2,0},{3,1},{4,6},{5,7},{6,4},{7,5},{8,72},{9,73},{10,... | collective-permute-start | bytes 786440 | tf_op jit(solution)/shard_map/ppermute | solution.py:338
  45.9 7.8 %collective-permute-start.13 = (f32[2,2,128,128]{3,2,1,0:T(8,128)S(1)}, f32[2,2,128,128]{3,2,1,0:T(8,128)}, u32[]{:S(2)}, u32[]{:S(2)}) collective-permute-start(f32[2,2,128,128]{3,2,1,0:T(8,128)S(1)} %get-tuple-element.41), channel_id=1, source_target_pairs={{0,3},{1,0},{2,1},{3,2},{4,7},{5,4},{6,5},{7,6},{8,104},{9,105},{1... | collective-permute-start | bytes 786440 | tf_op jit(solution)/shard_map/ppermute | solution.py:338
  54.8 5.8 %collective-permute-start.15 = (f32[2,128,128]{2,1,0:T(8,128)S(1)}, f32[2,128,128]{2,1,0:T(8,128)S(1)}, u32[]{:S(2)}, u32[]{:S(2)}) collective-permute-start(f32[2,128,128]{2,1,0:T(8,128)S(1)} %get-tuple-element.42), channel_id=1, source_target_pairs={{0,20},{1,21},{2,22},{3,23},{4,0},{5,1},{6,2},{7,3},{8,28},{9,29},... | collective-permute-start | bytes 393224 | tf_op jit(solution)/shard_map/ppermute | solution.py:338
  58.6 6.4 %collective-permute-start.14 = (f32[2,128,128]{2,1,0:T(8,128)S(1)}, f32[2,128,128]{2,1,0:T(8,128)S(1)}, u32[]{:S(2)}, u32[]{:S(2)}) collective-permute-start(f32[2,128,128]{2,1,0:T(8,128)S(1)} %get-tuple-element.42), channel_id=1, source_target_pairs={{0,4},{1,5},{2,6},{3,7},{4,16},{5,17},{6,18},{7,19},{8,12},{9,13},... | collective-permute-start | bytes 393224 | tf_op jit(solution)/shard_map/ppermute | solution.py:338
  58.7 6.4 %collective-permute-start.16 = (f32[2,128,128]{2,1,0:T(8,128)S(1)}, f32[2,128,128]{2,1,0:T(8,128)S(1)}, u32[]{:S(2)}, u32[]{:S(2)}) collective-permute-start(f32[2,128,128]{2,1,0:T(8,128)S(1)} %get-tuple-element.43), channel_id=1, source_target_pairs={{0,16},{1,17},{2,18},{3,19},{4,20},{5,21},{6,22},{7,23},{8,24},{9,... | collective-permute-start | bytes 393224 | tf_op jit(solution)/shard_map/ppermute | solution.py:338
  65.1 7.7 %collective-permute-start.19 = (f32[2,128,128]{2,1,0:T(8,128)S(1)}, f32[2,128,128]{2,1,0:T(8,128)S(1)}, u32[]{:S(2)}, u32[]{:S(2)}) collective-permute-start(f32[2,128,128]{2,1,0:T(8,128)S(1)} %add_add_fusion.1.rest_0_), channel_id=1, source_target_pairs={{0,96},{1,97},{2,98},{3,99},{4,100},{5,101},{6,102},{7,103},{8,104... | collective-permute-start | bytes 393224 | tf_op jit(solution)/shard_map/ppermute | solution.py:338
  67.5 8.3 %collective-permute-start.18 = (f32[2,128,128]{2,1,0:T(8,128)S(1)}, f32[2,128,128]{2,1,0:T(8,128)S(1)}, u32[]{:S(2)}, u32[]{:S(2)}) collective-permute-start(f32[2,128,128]{2,1,0:T(8,128)S(1)} %add_add_fusion.1.rest_0_), channel_id=1, source_target_pairs={{0,64},{1,65},{2,66},{3,67},{4,68},{5,69},{6,70},{7,71},{8,72},{9,... | collective-permute-start | bytes 393224 | tf_op jit(solution)/shard_map/ppermute | solution.py:338
  67.6 10.9 %collective-permute-start.17 = (f32[2,128,128]{2,1,0:T(8,128)S(1)}, f32[2,128,128]{2,1,0:T(8,128)S(1)}, u32[]{:S(2)}, u32[]{:S(2)}) collective-permute-start(f32[2,128,128]{2,1,0:T(8,128)S(1)} %add_add_fusion.1.rest_0_), channel_id=1, source_target_pairs={{0,32},{1,33},{2,34},{3,35},{4,36},{5,37},{6,38},{7,39},{8,40},{9,... | collective-permute-start | bytes 393224 | tf_op jit(solution)/shard_map/ppermute | solution.py:338
  68.2 11.5 %collective-permute-start.20 = (f32[2,128,128]{2,1,0:T(8,128)S(1)}, f32[2,128,128]{2,1,0:T(8,128)S(1)}, u32[]{:S(2)}, u32[]{:S(2)}) collective-permute-start(f32[2,128,128]{2,1,0:T(8,128)S(1)} %add_add_fusion.1.rest_0_), channel_id=1, source_target_pairs={{0,8},{8,0},{1,9},{9,1},{2,10},{10,2},{3,11},{11,3},{4,12},{12,4},... | collective-permute-start | bytes 393224 | tf_op jit(solution)/shard_map/ppermute | solution.py:342
  72.9 6.8 %collective-permute-start.23 = (f32[2,128,128]{2,1,0:T(8,128)S(1)}, f32[2,128,128]{2,1,0:T(8,128)S(1)}, u32[]{:S(2)}, u32[]{:S(2)}) collective-permute-start(f32[2,128,128]{2,1,0:T(8,128)S(1)} %collective-permute-done.19.rest_3_), channel_id=1, source_target_pairs={{0,8},{8,0},{1,9},{9,1},{2,10},{10,2},{3,11},{11,3},{4,12},{12,4},... | collective-permute-start | bytes 393224 | tf_op jit(solution)/shard_map/ppermute | solution.py:342
  75.8 3.9 %collective-permute-start.22 = (f32[2,128,128]{2,1,0:T(8,128)S(1)}, f32[2,128,128]{2,1,0:T(8,128)S(1)}, u32[]{:S(2)}, u32[]{:S(2)}) collective-permute-start(f32[2,128,128]{2,1,0:T(8,128)S(1)} %collective-permute-done.18.rest_2_), channel_id=1, source_target_pairs={{0,8},{8,0},{1,9},{9,1},{2,10},{10,2},{3,11},{11,3},{4,12},{12,4},... | collective-permute-start | bytes 393224 | tf_op jit(solution)/shard_map/ppermute | solution.py:342
  78.5 2.2 %collective-permute-start.21 = (f32[2,128,128]{2,1,0:T(8,128)S(1)}, f32[2,128,128]{2,1,0:T(8,128)S(1)}, u32[]{:S(2)}, u32[]{:S(2)}) collective-permute-start(f32[2,128,128]{2,1,0:T(8,128)S(1)} %collective-permute-done.17.rest_1_), channel_id=1, source_target_pairs={{0,8},{8,0},{1,9},{9,1},{2,10},{10,2},{3,11},{11,3},{4,12},{12,4},... | collective-permute-start | bytes 393224 | tf_op jit(solution)/shard_map/ppermute | solution.py:342
  (7 other events, 236.9 us)

commit v2 on v1

--- a/solution.py
+++ b/solution.py
@@ -48,9 +48,22 @@
     return (base ^ (seed & ~low)) * jnp.int32(MIX_ONE)
 
 
-CHUNK = 2048
+CHUNK = 4096
 TILE = 64
 PIECE = 512
+LOW = TILE * R - 1
+FIRST, LAST = 0, 115
+
+
+def tile_table(seed):
+    local = lax.broadcasted_iota(jnp.int32, (TILE, R), 0) * R + lax.broadcasted_iota(
+        jnp.int32, (TILE, R), 1
+    )
+    return first_mix(local, LOW, seed)
+
+
+def basis_tile(table, seed, row):
+    return finish(table + base_mix(row * R, LOW, seed))
 
 
 def reduce_kernel(
@@ -67,44 +80,51 @@
     for i in range(chunks):
         for w in range(2):
             copy(w, i).start()
-    low = TILE * R - 1
-    local = lax.broadcasted_iota(jnp.int32, (TILE, R), 0) * R + lax.broadcasted_iota(
-        jnp.int32, (TILE, R), 1
-    )
     seeds = [seed_ref[0], seed_ref[1]]
-    tables = [first_mix(local, low, seed) for seed in seeds]
+    tables = [tile_table(seed) for seed in seeds]
     acc[...] = jnp.zeros_like(acc)
+    tiles = [(w, t) for w in range(2) for t in range(0, CHUNK, TILE)]
+    pieces = [(w, d) for w in range(2) for d in range(0, CHUNK, PIECE)]
+    due = [
+        max(0, min(len(pieces), -(-(n - FIRST) * len(pieces) // (LAST - FIRST))))
+        for n in range(len(tiles))
+    ]
 
     def step(i, fill, use):
-        if use is not None:
-            for w in range(2):
+        parts = [None, None]
+
+        def multiply(w, d):
+            if d == 0:
                 copy(w, i - 1).wait()
+            cols = pl.ds(pl.multiple_of((i - 1) * CHUNK + d, PIECE), PIECE)
+            product = jnp.dot(
+                held[w][:, cols], use[w, d : d + PIECE, :], preferred_element_type=F32
+            )
+            parts[w] = product if parts[w] is None else parts[w] + product
+
+        if fill is None:
+            for piece in pieces:
+                multiply(*piece)
+        else:
+            done = 0
+            for n, (w, t) in enumerate(tiles):
+                for piece in pieces[done : due[n]]:
+                    multiply(*piece)
+                done = due[n]
+                fill[w, t : t + TILE, :] = basis_tile(tables[w], seeds[w], i * CHUNK + t)
         for w in range(2):
-            part = None
-            for t in range(CHUNK // TILE):
-                if fill is not None:
-                    start = base_mix((i * CHUNK + t * TILE) * R, low, seeds[w])
-                    fill[w, t * TILE : (t + 1) * TILE, :] = finish(tables[w] + start)
-                if use is not None and (t + 1) * TILE % PIECE == 0:
-                    d = (t + 1) * TILE - PIECE
-                    cols = pl.ds(pl.multiple_of((i - 1) * CHUNK + d, PIECE), PIECE)
-                    product = jnp.dot(
-                        held[w][:, cols], use[w, d : d + PIECE, :], preferred_element_type=F32
-                    )
-                    part = product if part is None else part + product
-            if part is not None:
-                acc[w] += part
-
-    step(0, even, None)
+            acc[w] += parts[w]
+
+    for w, t in tiles:
+        even[w, t : t + TILE, :] = basis_tile(tables[w], seeds[w], t)
 
     def body(k, carry):
         step(2 * k + 1, odd, even)
         step(2 * k + 2, even, odd)
         return carry
 
-    lax.fori_loop(0, chunks // 2 - 1, body, 0)
-    step(chunks - 1, odd, even)
-    step(chunks, None, odd)
+    lax.fori_loop(0, chunks // 2, body, 0)
+    step(chunks, None, even)
     for w in range(2):
         out_ref[w] = acc[w].astype(BF16).astype(F32).T
 
@@ -130,7 +150,7 @@
         ],
         compiler_params=pltpu.CompilerParams(vmem_limit_bytes=50 * 2**20),
         cost_estimate=pl.CostEstimate(
-            flops=4 * rows * FF * R, bytes_accessed=4 * rows * FF, transcendentals=0
+            flops=20 * rows * FF * R, bytes_accessed=4 * rows * FF, transcendentals=0
         ),
         name="reduce_both",
     )(seeds, gate_cot, up_cot)
@@ -149,20 +169,20 @@
 
 def theirs_kernel(act_ref, *outs):
     x, _, core, _, y = place()
-    for k, out in enumerate(outs):
+    for i, out in enumerate(outs):
+        owner, k = (1 - core, i) if i < 4 else (core, 2)
         for n in range(8):
-            cols = pooled_columns(1 - core, x, y, k, n // 4, n % 4)
+            cols = pooled_columns(owner, x, y, k, n // 4, n % 4)
             out[:, n * 128 : (n + 1) * 128] = act_ref[:, cols].astype(F32)
 
 
-def pairs_kernel(act_ref, *rest):
+def pair_kernel(act_ref, far_ref, out_ref, *, k):
     x, _, core, _, y = place()
-    for k, (far, out) in enumerate(zip(rest[:3], rest[3:])):
-        rows = act_ref.shape[0]
-        for n in range(8):
-            cols = pooled_columns(core, x, y, k + 1, n // 4, n % 4)
-            out[:rows, n * 128 : (n + 1) * 128] = act_ref[:, cols].astype(F32)
-        out[rows:, :] = far[...]
+    rows = act_ref.shape[0]
+    for n in range(8):
+        cols = pooled_columns(core, x, y, k, n // 4, n % 4)
+        out_ref[:rows, n * 128 : (n + 1) * 128] = act_ref[:, cols].astype(F32)
+    out_ref[rows:, :] = far_ref[...]
 
 
 def rows_for(kernel, name, height, count, act, *far):
@@ -182,9 +202,9 @@
 def grad_kernel(act_ref, *rest):
     x, _, core, _, y = place()
     second_at = jnp.where(core == 0, y, x)
-    others = rest[:4]
-    reds = rest[4:8]
-    outs = rest[8:12]
+    others = rest[:5]
+    reds = rest[5:9]
+    outs = rest[9:13]
     left = jnp.concatenate(
         [
             jnp.concatenate(
@@ -222,7 +242,7 @@
 def partial_grads(act, others, reds):
     return pl.pallas_call(
         grad_kernel,
-        in_specs=[pl.BlockSpec(memory_space=pltpu.VMEM)] * 9,
+        in_specs=[pl.BlockSpec(memory_space=pltpu.VMEM)] * 10,
         out_specs=[pl.BlockSpec(memory_space=pltpu.VMEM)] * 4,
         out_shape=[jax.ShapeDtypeStruct((2, 2, 128, 128), F32)] * 4,
         compiler_params=pltpu.CompilerParams(vmem_limit_bytes=16 * 2**20),
@@ -231,6 +251,26 @@
         ),
         name="partial_grads",
     )(act, *others, *reds)
+
+
+def sum_kernel(*refs):
+    zl = lax.axis_index("zl").astype(jnp.int32)
+    here_ref, away_ref = refs[4:]
+    for ref, at in ((here_ref, zl), (away_ref, 1 - zl)):
+        for w in range(2):
+            ref[w] = (refs[0][w, at] + refs[1][w, at]) + (refs[2][w, at] + refs[3][w, at])
+
+
+def sum_second(parts):
+    return pl.pallas_call(
+        sum_kernel,
+        in_specs=[pl.BlockSpec(memory_space=pltpu.VMEM)] * 4,
+        out_specs=[pl.BlockSpec(memory_space=pltpu.VMEM)] * 2,
+        out_shape=[jax.ShapeDtypeStruct((2, 128, 128), F32)] * 2,
+        compiler_params=pltpu.CompilerParams(vmem_limit_bytes=4 * 2**20),
+        cost_estimate=pl.CostEstimate(flops=10**6, bytes_accessed=10**6, transcendentals=0),
+        name="sum_second",
+    )(*parts)
 
 
 def columns_kernel(seed_ref, out_ref):
@@ -263,66 +303,73 @@
     )(seeds)
 
 
-def update_kernel(
-    basis_ref, gf_ref, gs_ref, uf_ref, us_ref, *rest
-):
-    grads = rest[:8]
-    step_out = rest[8:10]
-    moment_out = rest[10:14]
-    step_v = rest[14:16]
-    moment_v = rest[16:20]
-    sems = rest[20]
+def update_kernel(basis_ref, gf_ref, gs_ref, uf_ref, us_ref, *rest, places, before):
+    count = len(places)
+    grads = rest[:count]
+    outs = rest[count + before : count + before + 6]
+    step_v, moment_v, direction_v, sems = rest[count + before + 6 :]
     firsts = (gf_ref, uf_ref)
     seconds = (gs_ref, us_ref)
     pending = []
     x, _, core, _, _ = place()
-    for i in range(8):
-        side = core if i < 4 else 1 - core
-        start = (side * 4 + lax.rem(x - i % 4 + 4, 4)) * 128
-        rows = pl.ds(pl.multiple_of(start, 128), 128)
-        for w in range(2):
+    starts = []
+    for k, other in places:
+        side = 1 - core if other else core
+        starts.append(pl.multiple_of((side * 4 + lax.rem(x - k + 4, 4)) * 128, 128))
+
+    def send_out(src, dst, start, sem):
+        copy = pltpu.make_async_copy(src, dst.at[pl.ds(start, 128), :], sem)
+        copy.start()
+        pending.append(copy)
+
+    for w in range(2):
+        for i, start in enumerate(starts):
+            rows = pl.ds(start, 128)
+            here = pl.ds(i * 128, 128)
             grad = grads[i][w].T * (1.0 / TOKENS)
             first_new = beta_one * firsts[w][rows, :] + (1.0 - beta_one) * grad
             second_new = beta_two * seconds[w][rows, :] + (1.0 - beta_two) * grad * grad
-            moment_v[2 * w][rows, :] = first_new
-            moment_v[2 * w + 1][rows, :] = second_new
-            direction = (
+            moment_v[w, 0, here, :] = first_new
+            moment_v[w, 1, here, :] = second_new
+            direction_v[w, here, :] = (
                 first_new / bias_one / (jnp.sqrt(second_new / bias_two) + epsilon)
             ).astype(BF16)
-            step_v[w][rows, :] = jnp.dot(
-                direction, basis_ref[w], preferred_element_type=F32
+            for m in range(2):
+                send_out(moment_v.at[w, m, here], outs[2 + 2 * w + m], start, sems.at[w, i, m])
+        for p in range(0, count, 2):
+            both = pl.ds(p * 128, 256)
+            step_v[w, both, :] = jnp.dot(
+                direction_v[w, both, :], basis_ref[w], preferred_element_type=F32
             ).astype(BF16)
-            n = 0
-            for src, dst in (
-                (step_v[w], step_out[w]),
-                (moment_v[2 * w], moment_out[2 * w]),
-                (moment_v[2 * w + 1], moment_out[2 * w + 1]),
-            ):
-                copy = pltpu.make_async_copy(src.at[rows, :], dst.at[rows, :], sems.at[i, w, n])
-                copy.start()
-                pending.append(copy)
-                n += 1
+            for i in (p, p + 1):
+                send_out(step_v.at[w, pl.ds(i * 128, 128)], outs[w], starts[i], sems.at[w, i, 2])
     for copy in pending:
         copy.wait()
 
 
-def update(basis, moments, grads):
+def update(basis, moments, grads, places, before=()):
     rows, cols = moments[0].shape[0], basis.shape[2]
-    return pl.pallas_call(
-        update_kernel,
-        in_specs=[pl.BlockSpec(memory_space=pltpu.VMEM)] * 13,
+    count = len(places)
+    return pl.pallas_call(
+        functools.partial(update_kernel, places=places, before=len(before)),
+        in_specs=[pl.BlockSpec(memory_space=pltpu.VMEM)] * (5 + count)
+        + [pl.BlockSpec(memory_space=pl.ANY)] * len(before),
         out_specs=[pl.BlockSpec(memory_space=pl.ANY)] * 6,
         out_shape=[jax.ShapeDtypeStruct((rows, cols), BF16)] * 2
         + [jax.ShapeDtypeStruct((rows, R), F32)] * 4,
-        scratch_shapes=[pltpu.VMEM((rows, cols), BF16)] * 2
-        + [pltpu.VMEM((rows, R), F32)] * 4
-        + [pltpu.SemaphoreType.DMA((8, 2, 3))],
+        scratch_shapes=[
+            pltpu.VMEM((2, 128 * count, cols), BF16),
+            pltpu.VMEM((2, 2, 128 * count, R), F32),
+            pltpu.VMEM((2, 128 * count, R), BF16),
+            pltpu.SemaphoreType.DMA((2, count, 3)),
+        ],
+        input_output_aliases={5 + count + n: n for n in range(len(before))},
         compiler_params=pltpu.CompilerParams(vmem_limit_bytes=16 * 2**20),
         cost_estimate=pl.CostEstimate(
-            flops=4 * rows * cols * R, bytes_accessed=12 * 2**20, transcendentals=0
+            flops=count * 4 * 10**8, bytes_accessed=count * 10**6, transcendentals=0
         ),
-        name="update",
-    )(basis, *moments, *grads)
+        name="update_%d" % count,
+    )(basis, *moments, *grads, *before)
 
 
 def send(value, to):
@@ -352,27 +399,34 @@
         return send(value, lambda x, z, c, y: (x, z, c, y + k) if c == 0 else (x + k, z, c, y))
 
     rows = act.shape[0]
-    swapped = [swap_core(v) for v in rows_for(theirs_kernel, "theirs", rows, 4, act)]
-    pairs = rows_for(pairs_kernel, "pairs", 2 * rows, 3, act, *swapped[1:])
-    moved = [pool(pairs[k - 1], k) for k in range(1, 4)]
+    shares = rows_for(theirs_kernel, "theirs", rows, 5, act)
+    near = pool(shares[4], 2)
+    swapped = [swap_core(share) for share in shares[:4]]
+    pairs = {
+        k: rows_for(
+            functools.partial(pair_kernel, k=k), "pair_%d" % k, 2 * rows, 1, act, swapped[k]
+        )[0]
+        for k in (1, 3)
+    }
+    pairs[2] = swapped[2]
+    moved = {k: pool(pairs[k], k) for k in (1, 3, 2)}
 
     basis = basis_columns(seeds, FF // 16)
 
-    late_seeds, pairs = lax.optimization_barrier((seeds, pairs))
+    late_seeds, pairs, swapped[0] = lax.optimization_barrier((seeds, pairs, swapped[0]))
     reduced = reduce_both(late_seeds, gate_cot, up_cot)
     pair = jnp.stack([reduced, swap_core(reduced)])
+    pair, near = lax.optimization_barrier((pair, near))
     pooled = [pool(pair, k) for k in (1, 2)]
-    last, moved = lax.optimization_barrier((pair, moved))
+    last, moved[1], moved[3] = lax.optimization_barrier((pair, moved[1], moved[3]))
     pooled.append(pool(last, 3))
 
-    parts = partial_grads(act, [swapped[0]] + moved, [pair] + pooled)
+    others = [swapped[0], moved[1], near, moved[2], moved[3]]
+    parts = partial_grads(act, others, [pair] + pooled)
 
     mine, basis = lax.optimization_barrier((parts[0], basis))
-    for k in range(1, 4):
-        mine = mine + across(parts[k], k)
-
-    away = lax.dynamic_index_in_dim(mine, 1 - zl, 1, keepdims=False)
-    here = lax.dynamic_index_in_dim(mine, zl, 1, keepdims=False)
+    here, away = sum_second([mine] + [across(parts[k], k) for k in (2, 1, 3)])
+
     done = here + send(away, lambda x, z, c, y: (x, z + 1, c, y))
     done = done + send(away, lambda x, z, c, y: (x, z - 1, c, y))
     done = done + send(here, lambda x, z, c, y: (x, z + 2, c, y))
@@ -380,12 +434,11 @@
     own = [done] + [
         send(done, lambda x, z, c, y, k=k: (x + k, z, c, y)) for k in range(1, 4)
     ]
-    theirs = [swap_core(piece) for piece in own]
-    gate_step, up_step, gfn, gsn, ufn, usn = update(
-        basis,
-        (gate_first, gate_second, up_first, up_second),
-        own + theirs,
-    )
+    moments = (gate_first, gate_second, up_first, up_second)
+    places = tuple((k, other) for k in range(4) for other in (False, True))
+    grads = [swap_core(own[k]) if other else own[k] for k, other in places]
+    outs = update(basis, moments, grads, places)
+    gate_step, up_step, gfn, gsn, ufn, usn = outs
     return gate_step, up_step, gfn, gsn, ufn, usn
 
 

time: 85.4 us -> 79.8 us (0.934)
  waiting for transfers between devices: 20.1 us -> 15 us
  starting transfers between devices: 37.2 us -> 38.3 us
  other arithmetic: 1.14 us -> 0.05 us
    ppermute x15 -> x16, starting transfers between devices: 22.5 us -> 25.7 us  [send(): return lax.ppermute(value, AXES, perm)]
    ppermute x9, waiting for transfers between devices: 4.77 us -> 1.98 us  [swap_core(): return lax.ppermute(value, 'core', [(0, 1), (1, 0)])]
    ppermute x15 -> x16, waiting for transfers between devices: 15.3 us -> 13 us  [send(): return lax.ppermute(value, AXES, perm)]
    ppermute x9, starting transfers between devices: 14.7 us -> 12.6 us  [swap_core(): return lax.ppermute(value, 'core', [(0, 1), (1, 0)])]
    add x1 -> x0, other arithmetic: 1.09 us -> none  [local(): mine = mine + across(parts[k], k)]
    pallas_call x1 -> x2, Pallas kernels: 4.4 us -> 4.47 us  [the longest x1 4.41 us: update(): pl.pallas_call(functools.partial(update_kernel, places=places, before=len...]
  transfers between devices with their start and end apart: 24 -> 25, of which waited for: 12 -> 10; matrix products, arithmetic and copies ran while one was open for 0% -> 0% of each run, Pallas kernels for 22% -> 23%
where the time goes in v2:
time: 79.8 us; the launch traced here: 79.7 us
  starting transfers between devices  38.3 us (48%)
  Pallas kernels  23.8 us (30%)
  waiting for transfers between devices  15 us (19%)
  local copies, waits for them, and re-layouts  1.62 us (2%)
  between operations  0.93 us (1%)
    ppermute x16, starting transfers between devices, send(): return lax.ppermute(value, AXES, perm)  25.7 us
    pallas_call x1, Pallas kernels, reduce_both(): pl.pallas_call(reduce_kernel, in_specs=[pl.BlockSpec(memory_space=pltpu.S...  16.6 us
    ppermute x16, waiting for transfers between devices, send(): return lax.ppermute(value, AXES, perm)  13 us
    ppermute x9, starting transfers between devices, swap_core(): return lax.ppermute(value, 'core', [(0, 1), (1, 0)])  12.6 us
    pallas_call x1, Pallas kernels, update(): pl.pallas_call(functools.partial(update_kernel, places=places, before=len...  4.41 us
    ppermute x9, waiting for transfers between devices, swap_core(): return lax.ppermute(value, 'core', [(0, 1), (1, 0)])  1.98 us
    unnamed x14, local copies, waits for them, and re-layouts  1.62 us
  transfers between devices with their start and end apart: 25, of which 10 were waited for; matrix products, arithmetic and copies ran while one was open for 0% of the time, Pallas kernels for 23%

profile of v2, /device:TPU:1, one launch (start us, length us, event | category | flops | bytes accessed | tf_op | source)
XLA Modules:
  0.0 79.7 jit_solution(10770414784103178768)
XLA Ops:
  0.6 1.6 %copy-done = bf16[128,8192]{1,0:T(8,128)(2,1)S(1)} copy-done((bf16[128,8192]{1,0:T(8,128)(2,1)S(1)}, bf16[128,8192]{1,0:T(8,128)(2,1)}, u32[]{:S(2)}) %copy-start) | copy-done | bytes 2097176
  2.6 1.5 %collective-permute-start.2 = (f32[128,1024]{1,0:T(8,128)S(1)}, f32[128,1024]{1,0:T(8,128)S(1)}, u32[]{:S(2)}, u32[]{:S(2)}) collective-permute-start(f32[128,1024]{1,0:T(8,128)S(1)} %get-tuple-element.28), channel_id=1, source_target_pairs={{0,8},{8,0},{1,9},{9,1},{2,10},{10,2},{3,11},{11,3},{4,12},{12,4},... | collective-permute-start | bytes 1572872 | tf_op jit(solution)/shard_map/ppermute | solution.py:389
  4.7 3.0 %collective-permute-start.5 = (f32[128,1024]{1,0:T(8,128)S(1)}, f32[128,1024]{1,0:T(8,128)S(1)}, u32[]{:S(2)}, u32[]{:S(2)}) collective-permute-start(f32[128,1024]{1,0:T(8,128)S(1)} %get-tuple-element.32), channel_id=1, source_target_pairs={{0,64},{1,65},{2,66},{3,67},{4,68},{5,69},{6,70},{7,71},{8,10},{9,... | collective-permute-start | bytes 1572872 | tf_op jit(solution)/shard_map/ppermute | solution.py:385
  9.5 1.3 %collective-permute-start.8 = (f32[128,1024]{1,0:T(8,128)S(1)}, f32[128,1024]{1,0:T(8,128)S(1)}, u32[]{:S(2)}, u32[]{:S(2)}) collective-permute-start(f32[128,1024]{1,0:T(8,128)S(1)} %collective-permute-done.1), channel_id=1, source_target_pairs={{0,64},{1,65},{2,66},{3,67},{4,68},{5,69},{6,70},{7,71},{8,10},{9,... | collective-permute-start | bytes 1572872 | tf_op jit(solution)/shard_map/ppermute | solution.py:385
  10.9 16.6 %reduce_both.1 = f32[2,128,128]{2,1,0:T(8,128)S(1)} custom-call(s32[2]{0:T(128)S(1)} %copy-done.2, bf16[128,28672]{1,0:T(8,128)(2,1)} %gate_hbm.1, bf16[128,28672]{1,0:T(8,128)(2,1)} %up_hbm.1), custom_call_target="tpu_custom_call" | custom-call | flops 9395240960 | bytes 14680064 | tf_op jit(solution)/shard_map/reduce_both/pallas_call | solution.py:134
  29.3 3.0 %collective-permute-start.10 = (f32[2,2,128,128]{3,2,1,0:T(8,128)S(1)}, f32[2,2,128,128]{3,2,1,0:T(8,128)S(1)}, u32[]{:S(2)}, u32[]{:S(2)}) collective-permute-start(f32[2,2,128,128]{3,2,1,0:T(8,128)S(1)} %pad_maximum_fusion.rest_5_), channel_id=1, source_target_pairs={{0,64},{1,65},{2,66},{3,67},{4,68},{5,69},{6,70},{7,71},{8,10},{9,... | collective-permute-start | bytes 786440 | tf_op jit(solution)/shard_map/ppermute | solution.py:385
  32.7 2.3 %collective-permute-start.11 = (f32[2,2,128,128]{3,2,1,0:T(8,128)S(1)}, f32[2,2,128,128]{3,2,1,0:T(8,128)S(1)}, u32[]{:S(2)}, u32[]{:S(2)}) collective-permute-start(f32[2,2,128,128]{3,2,1,0:T(8,128)S(1)} %pad_maximum_fusion.rest_5_), channel_id=1, source_target_pairs={{0,96},{1,97},{2,98},{3,99},{4,100},{5,101},{6,102},{7,103},{8,11}... | collective-permute-start | bytes 786440 | tf_op jit(solution)/shard_map/ppermute | solution.py:385
  34.9 1.4 %collective-permute-done.10.rest_7_ = f32[2,2,128,128]{3,2,1,0:T(8,128)S(1)} collective-permute-done((f32[2,2,128,128]{3,2,1,0:T(8,128)S(1)}, f32[2,2,128,128]{3,2,1,0:T(8,128)S(1)}, u32[]{:S(2)}, u32[]{:S(2)}) %collective-permute-start.10) | collective-permute-done | bytes 262176 | tf_op jit(solution)/shard_map/ppermute | solution.py:385
  36.4 2.8 %collective-permute-done.9.rest_6_ = f32[2,2,128,128]{3,2,1,0:T(8,128)S(1)} collective-permute-done((f32[2,2,128,128]{3,2,1,0:T(8,128)S(1)}, f32[2,2,128,128]{3,2,1,0:T(8,128)S(1)}, u32[]{:S(2)}, u32[]{:S(2)}) %collective-permute-start.9) | collective-permute-done | bytes 262176 | tf_op jit(solution)/shard_map/ppermute | solution.py:385
  40.5 2.4 %collective-permute-start.12 = (f32[2,2,128,128]{3,2,1,0:T(8,128)S(1)}, f32[2,2,128,128]{3,2,1,0:T(8,128)S(1)}, u32[]{:S(2)}, u32[]{:S(2)}) collective-permute-start(f32[2,2,128,128]{3,2,1,0:T(8,128)S(1)} %get-tuple-element.41), channel_id=1, source_target_pairs={{0,2},{1,3},{2,0},{3,1},{4,6},{5,7},{6,4},{7,5},{8,72},{9,73},{10,... | collective-permute-start | bytes 786440 | tf_op jit(solution)/shard_map/ppermute | solution.py:385
  43.2 2.3 %collective-permute-start.14 = (f32[2,2,128,128]{3,2,1,0:T(8,128)S(1)}, f32[2,2,128,128]{3,2,1,0:T(8,128)S(1)}, u32[]{:S(2)}, u32[]{:S(2)}) collective-permute-start(f32[2,2,128,128]{3,2,1,0:T(8,128)S(1)} %get-tuple-element.43), channel_id=1, source_target_pairs={{0,3},{1,0},{2,1},{3,2},{4,7},{5,4},{6,5},{7,6},{8,104},{9,105},{1... | collective-permute-start | bytes 786440 | tf_op jit(solution)/shard_map/ppermute | solution.py:385
  45.6 1.2 %basis_columns.1.basis_ref = bf16[2,128,1792]{2,1,0:T(8,128)(2,1)S(1)} custom-call(s32[2]{0:T(128)S(1)} %copy-done.2), custom_call_target="tpu_custom_call" | custom-call | flops 9175040 | bytes 917504 | tf_op jit(solution)/shard_map/basis_columns/pallas_call | solution.py:293
  47.6 2.8 %collective-permute-done.13.refs_2_ = f32[2,2,128,128]{3,2,1,0:T(8,128)S(1)} collective-permute-done((f32[2,2,128,128]{3,2,1,0:T(8,128)S(1)}, f32[2,2,128,128]{3,2,1,0:T(8,128)S(1)}, u32[]{:S(2)}, u32[]{:S(2)}) %collective-permute-start.13) | collective-permute-done | bytes 262176 | tf_op jit(solution)/shard_map/ppermute | solution.py:385
  50.4 3.7 %collective-permute-start.17 = (f32[2,128,128]{2,1,0:T(8,128)S(1)}, f32[2,128,128]{2,1,0:T(8,128)S(1)}, u32[]{:S(2)}, u32[]{:S(2)}) collective-permute-start(f32[2,128,128]{2,1,0:T(8,128)S(1)} %get-tuple-element.44), channel_id=1, source_target_pairs={{0,16},{1,17},{2,18},{3,19},{4,20},{5,21},{6,22},{7,23},{8,24},{9,... | collective-permute-start | bytes 393224 | tf_op jit(solution)/shard_map/ppermute | solution.py:385
  54.5 1.0 %collective-permute-start.15 = (f32[2,128,128]{2,1,0:T(8,128)S(1)}, f32[2,128,128]{2,1,0:T(8,128)S(1)}, u32[]{:S(2)}, u32[]{:S(2)}) collective-permute-start(f32[2,128,128]{2,1,0:T(8,128)S(1)} %get-tuple-element.45), channel_id=1, source_target_pairs={{0,4},{1,5},{2,6},{3,7},{4,16},{5,17},{6,18},{7,19},{8,12},{9,13},... | collective-permute-start | bytes 393224 | tf_op jit(solution)/shard_map/ppermute | solution.py:385
  56.5 2.7 %collective-permute-done.16 = f32[2,128,128]{2,1,0:T(8,128)S(1)} collective-permute-done((f32[2,128,128]{2,1,0:T(8,128)S(1)}, f32[2,128,128]{2,1,0:T(8,128)S(1)}, u32[]{:S(2)}, u32[]{:S(2)}) %collective-permute-start.16) | collective-permute-done | bytes 131104 | tf_op jit(solution)/shard_map/ppermute | solution.py:385
  59.2 1.3 %collective-permute-done.15 = f32[2,128,128]{2,1,0:T(8,128)S(1)} collective-permute-done((f32[2,128,128]{2,1,0:T(8,128)S(1)}, f32[2,128,128]{2,1,0:T(8,128)S(1)}, u32[]{:S(2)}, u32[]{:S(2)}) %collective-permute-start.15) | collective-permute-done | bytes 131104 | tf_op jit(solution)/shard_map/ppermute | solution.py:385
  60.5 2.5 %collective-permute-start.23 = (f32[2,128,128]{2,1,0:T(8,128)S(1)}, f32[2,128,128]{2,1,0:T(8,128)S(1)}, u32[]{:S(2)}, u32[]{:S(2)}) collective-permute-start(f32[2,128,128]{2,1,0:T(8,128)S(1)} %add_add_fusion.rest_0_), channel_id=1, source_target_pairs={{0,96},{1,97},{2,98},{3,99},{4,100},{5,101},{6,102},{7,103},{8,104... | collective-permute-start | bytes 393224 | tf_op jit(solution)/shard_map/ppermute | solution.py:385
  63.0 1.4 %collective-permute-start.21 = (f32[2,128,128]{2,1,0:T(8,128)S(1)}, f32[2,128,128]{2,1,0:T(8,128)S(1)}, u32[]{:S(2)}, u32[]{:S(2)}) collective-permute-start(f32[2,128,128]{2,1,0:T(8,128)S(1)} %add_add_fusion.rest_0_), channel_id=1, source_target_pairs={{0,64},{1,65},{2,66},{3,67},{4,68},{5,69},{6,70},{7,71},{8,72},{9,... | collective-permute-start | bytes 393224 | tf_op jit(solution)/shard_map/ppermute | solution.py:385
  64.4 3.5 %collective-permute-start.18 = (f32[2,128,128]{2,1,0:T(8,128)S(1)}, f32[2,128,128]{2,1,0:T(8,128)S(1)}, u32[]{:S(2)}, u32[]{:S(2)}) collective-permute-start(f32[2,128,128]{2,1,0:T(8,128)S(1)} %add_add_fusion.rest_0_), channel_id=1, source_target_pairs={{0,8},{8,0},{1,9},{9,1},{2,10},{10,2},{3,11},{11,3},{4,12},{12,4},... | collective-permute-start | bytes 393224 | tf_op jit(solution)/shard_map/ppermute | solution.py:389
  67.9 2.3 %collective-permute-start.24 = (f32[2,128,128]{2,1,0:T(8,128)S(1)}, f32[2,128,128]{2,1,0:T(8,128)S(1)}, u32[]{:S(2)}, u32[]{:S(2)}) collective-permute-start(f32[2,128,128]{2,1,0:T(8,128)S(1)} %collective-permute-done.23.rest_6_), channel_id=1, source_target_pairs={{0,8},{8,0},{1,9},{9,1},{2,10},{10,2},{3,11},{11,3},{4,12},{12,4},... | collective-permute-start | bytes 393224 | tf_op jit(solution)/shard_map/ppermute | solution.py:389
  70.2 2.5 %collective-permute-start.22 = (f32[2,128,128]{2,1,0:T(8,128)S(1)}, f32[2,128,128]{2,1,0:T(8,128)S(1)}, u32[]{:S(2)}, u32[]{:S(2)}) collective-permute-start(f32[2,128,128]{2,1,0:T(8,128)S(1)} %collective-permute-done.21.rest_4_), channel_id=1, source_target_pairs={{0,8},{8,0},{1,9},{9,1},{2,10},{10,2},{3,11},{11,3},{4,12},{12,4},... | collective-permute-start | bytes 393224 | tf_op jit(solution)/shard_map/ppermute | solution.py:389
  72.7 1.4 %collective-permute-start.20 = (f32[2,128,128]{2,1,0:T(8,128)S(1)}, f32[2,128,128]{2,1,0:T(8,128)S(1)}, u32[]{:S(2)}, u32[]{:S(2)}) collective-permute-start(f32[2,128,128]{2,1,0:T(8,128)S(1)} %collective-permute-done.19.rest_2_), channel_id=1, source_target_pairs={{0,8},{8,0},{1,9},{9,1},{2,10},{10,2},{3,11},{11,3},{4,12},{12,4},... | collective-permute-start | bytes 393224 | tf_op jit(solution)/shard_map/ppermute | solution.py:389
  75.1 4.4 %update_8.1 = (bf16[1024,1792]{1,0:T(8,128)(2,1)}, bf16[1024,1792]{1,0:T(8,128)(2,1)}, f32[1024,128]{1,0:T(8,128)}, f32[1024,128]{1,0:T(8,128)}, f32[1024,128]{1,0:T(8,128)}, /*index=5*/f32[1024,128]{1,0:T(8,128)}) custom-call(bf16[2,128,1792]{2,1,0:T(8,128)(2,1)S(1)} %basis_columns.1.basis_ref, f32[1024,128]{1,0:T(8,128)S(1)} %copy-done.3, ...), custom_call_target="tpu_custom_call" | custom-call | flops 3200000000 | bytes 8000000 | tf_op jit(solution)/shard_map/update_8/pallas_call | solution.py:353
  (50 shorter events, 9.7 us)
Async XLA Ops:
  2.6 5.1 %collective-permute-start.2 = (f32[128,1024]{1,0:T(8,128)S(1)}, f32[128,1024]{1,0:T(8,128)S(1)}, u32[]{:S(2)}, u32[]{:S(2)}) collective-permute-start(f32[128,1024]{1,0:T(8,128)S(1)} %get-tuple-element.28), channel_id=1, source_target_pairs={{0,8},{8,0},{1,9},{9,1},{2,10},{10,2},{3,11},{11,3},{4,12},{12,4},... | collective-permute-start | bytes 1572872 | tf_op jit(solution)/shard_map/ppermute | solution.py:389
  4.1 4.6 %collective-permute-start = (f32[128,1024]{1,0:T(8,128)S(1)}, f32[128,1024]{1,0:T(8,128)S(1)}, u32[]{:S(2)}, u32[]{:S(2)}) collective-permute-start(f32[128,1024]{1,0:T(8,128)S(1)} %get-tuple-element.26), channel_id=1, source_target_pairs={{0,8},{8,0},{1,9},{9,1},{2,10},{10,2},{3,11},{11,3},{4,12},{12,4},... | collective-permute-start | bytes 1572872 | tf_op jit(solution)/shard_map/ppermute | solution.py:389
  4.2 5.4 %collective-permute-start.1 = (f32[128,1024]{1,0:T(8,128)S(1)}, f32[128,1024]{1,0:T(8,128)S(1)}, u32[]{:S(2)}, u32[]{:S(2)}) collective-permute-start(f32[128,1024]{1,0:T(8,128)S(1)} %get-tuple-element.27), channel_id=1, source_target_pairs={{0,8},{8,0},{1,9},{9,1},{2,10},{10,2},{3,11},{11,3},{4,12},{12,4},... | collective-permute-start | bytes 1572872 | tf_op jit(solution)/shard_map/ppermute | solution.py:389
  4.6 4.9 %collective-permute-start.3 = (f32[128,1024]{1,0:T(8,128)S(1)}, f32[128,1024]{1,0:T(8,128)S(1)}, u32[]{:S(2)}, u32[]{:S(2)}) collective-permute-start(f32[128,1024]{1,0:T(8,128)S(1)} %get-tuple-element.29), channel_id=1, source_target_pairs={{0,8},{8,0},{1,9},{9,1},{2,10},{10,2},{3,11},{11,3},{4,12},{12,4},... | collective-permute-start | bytes 1572872 | tf_op jit(solution)/shard_map/ppermute | solution.py:389
  4.7 24.6 %collective-permute-start.5 = (f32[128,1024]{1,0:T(8,128)S(1)}, f32[128,1024]{1,0:T(8,128)S(1)}, u32[]{:S(2)}, u32[]{:S(2)}) collective-permute-start(f32[128,1024]{1,0:T(8,128)S(1)} %get-tuple-element.32), channel_id=1, source_target_pairs={{0,64},{1,65},{2,66},{3,67},{4,68},{5,69},{6,70},{7,71},{8,10},{9,... | collective-permute-start | bytes 1572872 | tf_op jit(solution)/shard_map/ppermute | solution.py:385
  7.8 24.8 %collective-permute-start.7 = (f32[256,1024]{1,0:T(8,128)S(1)}, f32[256,1024]{1,0:T(8,128)S(1)}, u32[]{:S(2)}, u32[]{:S(2)}) collective-permute-start(f32[256,1024]{1,0:T(8,128)S(1)} %pair_3.1), channel_id=1, source_target_pairs={{0,96},{1,97},{2,98},{3,99},{4,100},{5,101},{6,102},{7,103},{8,11}... | collective-permute-start | bytes 3145736 | tf_op jit(solution)/shard_map/ppermute | solution.py:385
  8.8 23.9 %collective-permute-start.6 = (f32[256,1024]{1,0:T(8,128)S(1)}, f32[256,1024]{1,0:T(8,128)S(1)}, u32[]{:S(2)}, u32[]{:S(2)}) collective-permute-start(f32[256,1024]{1,0:T(8,128)S(1)} %pair_1.1), channel_id=1, source_target_pairs={{0,32},{1,33},{2,34},{3,35},{4,36},{5,37},{6,38},{7,39},{8,9},{9,1... | collective-permute-start | bytes 3145736 | tf_op jit(solution)/shard_map/ppermute | solution.py:385
  9.5 29.6 %collective-permute-start.8 = (f32[128,1024]{1,0:T(8,128)S(1)}, f32[128,1024]{1,0:T(8,128)S(1)}, u32[]{:S(2)}, u32[]{:S(2)}) collective-permute-start(f32[128,1024]{1,0:T(8,128)S(1)} %collective-permute-done.1), channel_id=1, source_target_pairs={{0,64},{1,65},{2,66},{3,67},{4,68},{5,69},{6,70},{7,71},{8,10},{9,... | collective-permute-start | bytes 1572872 | tf_op jit(solution)/shard_map/ppermute | solution.py:385
  29.3 7.1 %collective-permute-start.10 = (f32[2,2,128,128]{3,2,1,0:T(8,128)S(1)}, f32[2,2,128,128]{3,2,1,0:T(8,128)S(1)}, u32[]{:S(2)}, u32[]{:S(2)}) collective-permute-start(f32[2,2,128,128]{3,2,1,0:T(8,128)S(1)} %pad_maximum_fusion.rest_5_), channel_id=1, source_target_pairs={{0,64},{1,65},{2,66},{3,67},{4,68},{5,69},{6,70},{7,71},{8,10},{9,... | collective-permute-start | bytes 786440 | tf_op jit(solution)/shard_map/ppermute | solution.py:385
  32.2 6.9 %collective-permute-start.9 = (f32[2,2,128,128]{3,2,1,0:T(8,128)S(1)}, f32[2,2,128,128]{3,2,1,0:T(8,128)S(1)}, u32[]{:S(2)}, u32[]{:S(2)}) collective-permute-start(f32[2,2,128,128]{3,2,1,0:T(8,128)S(1)} %pad_maximum_fusion.rest_5_), channel_id=1, source_target_pairs={{0,32},{1,33},{2,34},{3,35},{4,36},{5,37},{6,38},{7,39},{8,9},{9,1... | collective-permute-start | bytes 786440 | tf_op jit(solution)/shard_map/ppermute | solution.py:385
  32.7 6.9 %collective-permute-start.11 = (f32[2,2,128,128]{3,2,1,0:T(8,128)S(1)}, f32[2,2,128,128]{3,2,1,0:T(8,128)S(1)}, u32[]{:S(2)}, u32[]{:S(2)}) collective-permute-start(f32[2,2,128,128]{3,2,1,0:T(8,128)S(1)} %pad_maximum_fusion.rest_5_), channel_id=1, source_target_pairs={{0,96},{1,97},{2,98},{3,99},{4,100},{5,101},{6,102},{7,103},{8,11}... | collective-permute-start | bytes 786440 | tf_op jit(solution)/shard_map/ppermute | solution.py:385
  40.5 7.1 %collective-permute-start.12 = (f32[2,2,128,128]{3,2,1,0:T(8,128)S(1)}, f32[2,2,128,128]{3,2,1,0:T(8,128)S(1)}, u32[]{:S(2)}, u32[]{:S(2)}) collective-permute-start(f32[2,2,128,128]{3,2,1,0:T(8,128)S(1)} %get-tuple-element.41), channel_id=1, source_target_pairs={{0,2},{1,3},{2,0},{3,1},{4,6},{5,7},{6,4},{7,5},{8,72},{9,73},{10,... | collective-permute-start | bytes 786440 | tf_op jit(solution)/shard_map/ppermute | solution.py:385
  42.9 7.5 %collective-permute-start.13 = (f32[2,2,128,128]{3,2,1,0:T(8,128)S(1)}, f32[2,2,128,128]{3,2,1,0:T(8,128)S(1)}, u32[]{:S(2)}, u32[]{:S(2)}) collective-permute-start(f32[2,2,128,128]{3,2,1,0:T(8,128)S(1)} %get-tuple-element.42), channel_id=1, source_target_pairs={{0,1},{1,2},{2,3},{3,0},{4,5},{5,6},{6,7},{7,4},{8,40},{9,41},{10,... | collective-permute-start | bytes 786440 | tf_op jit(solution)/shard_map/ppermute | solution.py:385
  43.2 7.2 %collective-permute-start.14 = (f32[2,2,128,128]{3,2,1,0:T(8,128)S(1)}, f32[2,2,128,128]{3,2,1,0:T(8,128)S(1)}, u32[]{:S(2)}, u32[]{:S(2)}) collective-permute-start(f32[2,2,128,128]{3,2,1,0:T(8,128)S(1)} %get-tuple-element.43), channel_id=1, source_target_pairs={{0,3},{1,0},{2,1},{3,2},{4,7},{5,4},{6,5},{7,6},{8,104},{9,105},{1... | collective-permute-start | bytes 786440 | tf_op jit(solution)/shard_map/ppermute | solution.py:385
  50.4 6.0 %collective-permute-start.17 = (f32[2,128,128]{2,1,0:T(8,128)S(1)}, f32[2,128,128]{2,1,0:T(8,128)S(1)}, u32[]{:S(2)}, u32[]{:S(2)}) collective-permute-start(f32[2,128,128]{2,1,0:T(8,128)S(1)} %get-tuple-element.44), channel_id=1, source_target_pairs={{0,16},{1,17},{2,18},{3,19},{4,20},{5,21},{6,22},{7,23},{8,24},{9,... | collective-permute-start | bytes 393224 | tf_op jit(solution)/shard_map/ppermute | solution.py:385
  54.1 5.1 %collective-permute-start.16 = (f32[2,128,128]{2,1,0:T(8,128)S(1)}, f32[2,128,128]{2,1,0:T(8,128)S(1)}, u32[]{:S(2)}, u32[]{:S(2)}) collective-permute-start(f32[2,128,128]{2,1,0:T(8,128)S(1)} %get-tuple-element.45), channel_id=1, source_target_pairs={{0,20},{1,21},{2,22},{3,23},{4,0},{5,1},{6,2},{7,3},{8,28},{9,29},... | collective-permute-start | bytes 393224 | tf_op jit(solution)/shard_map/ppermute | solution.py:385
  54.5 5.9 %collective-permute-start.15 = (f32[2,128,128]{2,1,0:T(8,128)S(1)}, f32[2,128,128]{2,1,0:T(8,128)S(1)}, u32[]{:S(2)}, u32[]{:S(2)}) collective-permute-start(f32[2,128,128]{2,1,0:T(8,128)S(1)} %get-tuple-element.45), channel_id=1, source_target_pairs={{0,4},{1,5},{2,6},{3,7},{4,16},{5,17},{6,18},{7,19},{8,12},{9,13},... | collective-permute-start | bytes 393224 | tf_op jit(solution)/shard_map/ppermute | solution.py:385
  60.5 7.4 %collective-permute-start.23 = (f32[2,128,128]{2,1,0:T(8,128)S(1)}, f32[2,128,128]{2,1,0:T(8,128)S(1)}, u32[]{:S(2)}, u32[]{:S(2)}) collective-permute-start(f32[2,128,128]{2,1,0:T(8,128)S(1)} %add_add_fusion.rest_0_), channel_id=1, source_target_pairs={{0,96},{1,97},{2,98},{3,99},{4,100},{5,101},{6,102},{7,103},{8,104... | collective-permute-start | bytes 393224 | tf_op jit(solution)/shard_map/ppermute | solution.py:385
  63.0 7.2 %collective-permute-start.21 = (f32[2,128,128]{2,1,0:T(8,128)S(1)}, f32[2,128,128]{2,1,0:T(8,128)S(1)}, u32[]{:S(2)}, u32[]{:S(2)}) collective-permute-start(f32[2,128,128]{2,1,0:T(8,128)S(1)} %add_add_fusion.rest_0_), channel_id=1, source_target_pairs={{0,64},{1,65},{2,66},{3,67},{4,68},{5,69},{6,70},{7,71},{8,72},{9,... | collective-permute-start | bytes 393224 | tf_op jit(solution)/shard_map/ppermute | solution.py:385
  64.4 8.4 %collective-permute-start.19 = (f32[2,128,128]{2,1,0:T(8,128)S(1)}, f32[2,128,128]{2,1,0:T(8,128)S(1)}, u32[]{:S(2)}, u32[]{:S(2)}) collective-permute-start(f32[2,128,128]{2,1,0:T(8,128)S(1)} %add_add_fusion.rest_0_), channel_id=1, source_target_pairs={{0,32},{1,33},{2,34},{3,35},{4,36},{5,37},{6,38},{7,39},{8,40},{9,... | collective-permute-start | bytes 393224 | tf_op jit(solution)/shard_map/ppermute | solution.py:385
  64.4 9.8 %collective-permute-start.18 = (f32[2,128,128]{2,1,0:T(8,128)S(1)}, f32[2,128,128]{2,1,0:T(8,128)S(1)}, u32[]{:S(2)}, u32[]{:S(2)}) collective-permute-start(f32[2,128,128]{2,1,0:T(8,128)S(1)} %add_add_fusion.rest_0_), channel_id=1, source_target_pairs={{0,8},{8,0},{1,9},{9,1},{2,10},{10,2},{3,11},{11,3},{4,12},{12,4},... | collective-permute-start | bytes 393224 | tf_op jit(solution)/shard_map/ppermute | solution.py:389
  67.9 6.3 %collective-permute-start.24 = (f32[2,128,128]{2,1,0:T(8,128)S(1)}, f32[2,128,128]{2,1,0:T(8,128)S(1)}, u32[]{:S(2)}, u32[]{:S(2)}) collective-permute-start(f32[2,128,128]{2,1,0:T(8,128)S(1)} %collective-permute-done.23.rest_6_), channel_id=1, source_target_pairs={{0,8},{8,0},{1,9},{9,1},{2,10},{10,2},{3,11},{11,3},{4,12},{12,4},... | collective-permute-start | bytes 393224 | tf_op jit(solution)/shard_map/ppermute | solution.py:389
  70.2 4.0 %collective-permute-start.22 = (f32[2,128,128]{2,1,0:T(8,128)S(1)}, f32[2,128,128]{2,1,0:T(8,128)S(1)}, u32[]{:S(2)}, u32[]{:S(2)}) collective-permute-start(f32[2,128,128]{2,1,0:T(8,128)S(1)} %collective-permute-done.21.rest_4_), channel_id=1, source_target_pairs={{0,8},{8,0},{1,9},{9,1},{2,10},{10,2},{3,11},{11,3},{4,12},{12,4},... | collective-permute-start | bytes 393224 | tf_op jit(solution)/shard_map/ppermute | solution.py:389
  72.7 2.4 %collective-permute-start.20 = (f32[2,128,128]{2,1,0:T(8,128)S(1)}, f32[2,128,128]{2,1,0:T(8,128)S(1)}, u32[]{:S(2)}, u32[]{:S(2)}) collective-permute-start(f32[2,128,128]{2,1,0:T(8,128)S(1)} %collective-permute-done.19.rest_2_), channel_id=1, source_target_pairs={{0,8},{8,0},{1,9},{9,1},{2,10},{10,2},{3,11},{11,3},{4,12},{12,4},... | collective-permute-start | bytes 393224 | tf_op jit(solution)/shard_map/ppermute | solution.py:389
  (8 other events, 223.8 us)

commit v3 on v2

--- a/solution.py
+++ b/solution.py
@@ -52,7 +52,7 @@
 TILE = 64
 PIECE = 512
 LOW = TILE * R - 1
-FIRST, LAST = 0, 115
+FIRST, LAST = 0, 124
 
 
 def tile_table(seed):
@@ -83,8 +83,8 @@
     seeds = [seed_ref[0], seed_ref[1]]
     tables = [tile_table(seed) for seed in seeds]
     acc[...] = jnp.zeros_like(acc)
-    tiles = [(w, t) for w in range(2) for t in range(0, CHUNK, TILE)]
-    pieces = [(w, d) for w in range(2) for d in range(0, CHUNK, PIECE)]
+    tiles = [(w, t) for t in range(0, CHUNK, TILE) for w in range(2)]
+    pieces = [(w, d) for d in range(0, CHUNK, PIECE) for w in range(2)]
     due = [
         max(0, min(len(pieces), -(-(n - FIRST) * len(pieces) // (LAST - FIRST))))
         for n in range(len(tiles))

time: 79.8 us -> 79.2 us (level)
  Pallas kernels: 23.8 us -> 23 us
  transfers between devices with their start and end apart: 25 -> 25, of which waited for: 10 -> 10; matrix products, arithmetic and copies ran while one was open for 0% -> 0% of each run, Pallas kernels for 23% -> 22%
where the time goes in v3:
time: 79.2 us; the launch traced here: 79.1 us
  starting transfers between devices  38.5 us (49%)
  Pallas kernels  23 us (29%)
  waiting for transfers between devices  15 us (19%)
  local copies, waits for them, and re-layouts  1.62 us (2%)
  between operations  0.93 us (1%)
    ppermute x16, starting transfers between devices, send(): return lax.ppermute(value, AXES, perm)  25.9 us
    pallas_call x1, Pallas kernels, reduce_both(): pl.pallas_call(reduce_kernel, in_specs=[pl.BlockSpec(memory_space=pltpu.S...  15.8 us
    ppermute x16, waiting for transfers between devices, send(): return lax.ppermute(value, AXES, perm)  13 us
    ppermute x9, starting transfers between devices, swap_core(): return lax.ppermute(value, 'core', [(0, 1), (1, 0)])  12.6 us
    pallas_call x1, Pallas kernels, update(): pl.pallas_call(functools.partial(update_kernel, places=places, before=len...  4.41 us
    ppermute x9, waiting for transfers between devices, swap_core(): return lax.ppermute(value, 'core', [(0, 1), (1, 0)])  1.98 us
    unnamed x14, local copies, waits for them, and re-layouts  1.62 us
  transfers between devices with their start and end apart: 25, of which 10 were waited for; matrix products, arithmetic and copies ran while one was open for 0% of the time, Pallas kernels for 22%

profile of v3, /device:TPU:1, one launch (start us, length us, event | category | flops | bytes accessed | tf_op | source)
XLA Modules:
  0.0 79.1 jit_solution(4164959620278790951)
XLA Ops:
  0.6 1.6 %copy-done = bf16[128,8192]{1,0:T(8,128)(2,1)S(1)} copy-done((bf16[128,8192]{1,0:T(8,128)(2,1)S(1)}, bf16[128,8192]{1,0:T(8,128)(2,1)}, u32[]{:S(2)}) %copy-start) | copy-done | bytes 2097176
  2.6 1.5 %collective-permute-start.2 = (f32[128,1024]{1,0:T(8,128)S(1)}, f32[128,1024]{1,0:T(8,128)S(1)}, u32[]{:S(2)}, u32[]{:S(2)}) collective-permute-start(f32[128,1024]{1,0:T(8,128)S(1)} %get-tuple-element.28), channel_id=1, source_target_pairs={{0,8},{8,0},{1,9},{9,1},{2,10},{10,2},{3,11},{11,3},{4,12},{12,4},... | collective-permute-start | bytes 1572872 | tf_op jit(solution)/shard_map/ppermute | solution.py:389
  4.7 3.0 %collective-permute-start.5 = (f32[128,1024]{1,0:T(8,128)S(1)}, f32[128,1024]{1,0:T(8,128)S(1)}, u32[]{:S(2)}, u32[]{:S(2)}) collective-permute-start(f32[128,1024]{1,0:T(8,128)S(1)} %get-tuple-element.32), channel_id=1, source_target_pairs={{0,64},{1,65},{2,66},{3,67},{4,68},{5,69},{6,70},{7,71},{8,10},{9,... | collective-permute-start | bytes 1572872 | tf_op jit(solution)/shard_map/ppermute | solution.py:385
  9.5 1.3 %collective-permute-start.8 = (f32[128,1024]{1,0:T(8,128)S(1)}, f32[128,1024]{1,0:T(8,128)S(1)}, u32[]{:S(2)}, u32[]{:S(2)}) collective-permute-start(f32[128,1024]{1,0:T(8,128)S(1)} %collective-permute-done.1), channel_id=1, source_target_pairs={{0,64},{1,65},{2,66},{3,67},{4,68},{5,69},{6,70},{7,71},{8,10},{9,... | collective-permute-start | bytes 1572872 | tf_op jit(solution)/shard_map/ppermute | solution.py:385
  10.9 15.8 %reduce_both.1 = f32[2,128,128]{2,1,0:T(8,128)S(1)} custom-call(s32[2]{0:T(128)S(1)} %copy-done.2, bf16[128,28672]{1,0:T(8,128)(2,1)} %gate_hbm.1, bf16[128,28672]{1,0:T(8,128)(2,1)} %up_hbm.1), custom_call_target="tpu_custom_call" | custom-call | flops 9395240960 | bytes 14680064 | tf_op jit(solution)/shard_map/reduce_both/pallas_call | solution.py:134
  28.5 3.0 %collective-permute-start.10 = (f32[2,2,128,128]{3,2,1,0:T(8,128)S(1)}, f32[2,2,128,128]{3,2,1,0:T(8,128)S(1)}, u32[]{:S(2)}, u32[]{:S(2)}) collective-permute-start(f32[2,2,128,128]{3,2,1,0:T(8,128)S(1)} %pad_maximum_fusion.rest_5_), channel_id=1, source_target_pairs={{0,64},{1,65},{2,66},{3,67},{4,68},{5,69},{6,70},{7,71},{8,10},{9,... | collective-permute-start | bytes 786440 | tf_op jit(solution)/shard_map/ppermute | solution.py:385
  31.9 2.3 %collective-permute-start.11 = (f32[2,2,128,128]{3,2,1,0:T(8,128)S(1)}, f32[2,2,128,128]{3,2,1,0:T(8,128)S(1)}, u32[]{:S(2)}, u32[]{:S(2)}) collective-permute-start(f32[2,2,128,128]{3,2,1,0:T(8,128)S(1)} %pad_maximum_fusion.rest_5_), channel_id=1, source_target_pairs={{0,96},{1,97},{2,98},{3,99},{4,100},{5,101},{6,102},{7,103},{8,11}... | collective-permute-start | bytes 786440 | tf_op jit(solution)/shard_map/ppermute | solution.py:385
  34.1 1.4 %collective-permute-done.10.rest_7_ = f32[2,2,128,128]{3,2,1,0:T(8,128)S(1)} collective-permute-done((f32[2,2,128,128]{3,2,1,0:T(8,128)S(1)}, f32[2,2,128,128]{3,2,1,0:T(8,128)S(1)}, u32[]{:S(2)}, u32[]{:S(2)}) %collective-permute-start.10) | collective-permute-done | bytes 262176 | tf_op jit(solution)/shard_map/ppermute | solution.py:385
  35.6 2.8 %collective-permute-done.9.rest_6_ = f32[2,2,128,128]{3,2,1,0:T(8,128)S(1)} collective-permute-done((f32[2,2,128,128]{3,2,1,0:T(8,128)S(1)}, f32[2,2,128,128]{3,2,1,0:T(8,128)S(1)}, u32[]{:S(2)}, u32[]{:S(2)}) %collective-permute-start.9) | collective-permute-done | bytes 262176 | tf_op jit(solution)/shard_map/ppermute | solution.py:385
  39.7 2.6 %collective-permute-start.12 = (f32[2,2,128,128]{3,2,1,0:T(8,128)S(1)}, f32[2,2,128,128]{3,2,1,0:T(8,128)S(1)}, u32[]{:S(2)}, u32[]{:S(2)}) collective-permute-start(f32[2,2,128,128]{3,2,1,0:T(8,128)S(1)} %get-tuple-element.41), channel_id=1, source_target_pairs={{0,2},{1,3},{2,0},{3,1},{4,6},{5,7},{6,4},{7,5},{8,72},{9,73},{10,... | collective-permute-start | bytes 786440 | tf_op jit(solution)/shard_map/ppermute | solution.py:385
  42.6 2.3 %collective-permute-start.14 = (f32[2,2,128,128]{3,2,1,0:T(8,128)S(1)}, f32[2,2,128,128]{3,2,1,0:T(8,128)S(1)}, u32[]{:S(2)}, u32[]{:S(2)}) collective-permute-start(f32[2,2,128,128]{3,2,1,0:T(8,128)S(1)} %get-tuple-element.43), channel_id=1, source_target_pairs={{0,3},{1,0},{2,1},{3,2},{4,7},{5,4},{6,5},{7,6},{8,104},{9,105},{1... | collective-permute-start | bytes 786440 | tf_op jit(solution)/shard_map/ppermute | solution.py:385
  45.0 1.2 %basis_columns.1.basis_ref = bf16[2,128,1792]{2,1,0:T(8,128)(2,1)S(1)} custom-call(s32[2]{0:T(128)S(1)} %copy-done.2), custom_call_target="tpu_custom_call" | custom-call | flops 9175040 | bytes 917504 | tf_op jit(solution)/shard_map/basis_columns/pallas_call | solution.py:293
  47.0 2.8 %collective-permute-done.13.refs_2_ = f32[2,2,128,128]{3,2,1,0:T(8,128)S(1)} collective-permute-done((f32[2,2,128,128]{3,2,1,0:T(8,128)S(1)}, f32[2,2,128,128]{3,2,1,0:T(8,128)S(1)}, u32[]{:S(2)}, u32[]{:S(2)}) %collective-permute-start.13) | collective-permute-done | bytes 262176 | tf_op jit(solution)/shard_map/ppermute | solution.py:385
  49.8 3.7 %collective-permute-start.17 = (f32[2,128,128]{2,1,0:T(8,128)S(1)}, f32[2,128,128]{2,1,0:T(8,128)S(1)}, u32[]{:S(2)}, u32[]{:S(2)}) collective-permute-start(f32[2,128,128]{2,1,0:T(8,128)S(1)} %get-tuple-element.44), channel_id=1, source_target_pairs={{0,16},{1,17},{2,18},{3,19},{4,20},{5,21},{6,22},{7,23},{8,24},{9,... | collective-permute-start | bytes 393224 | tf_op jit(solution)/shard_map/ppermute | solution.py:385
  53.9 1.0 %collective-permute-start.15 = (f32[2,128,128]{2,1,0:T(8,128)S(1)}, f32[2,128,128]{2,1,0:T(8,128)S(1)}, u32[]{:S(2)}, u32[]{:S(2)}) collective-permute-start(f32[2,128,128]{2,1,0:T(8,128)S(1)} %get-tuple-element.45), channel_id=1, source_target_pairs={{0,4},{1,5},{2,6},{3,7},{4,16},{5,17},{6,18},{7,19},{8,12},{9,13},... | collective-permute-start | bytes 393224 | tf_op jit(solution)/shard_map/ppermute | solution.py:385
  55.9 2.7 %collective-permute-done.16 = f32[2,128,128]{2,1,0:T(8,128)S(1)} collective-permute-done((f32[2,128,128]{2,1,0:T(8,128)S(1)}, f32[2,128,128]{2,1,0:T(8,128)S(1)}, u32[]{:S(2)}, u32[]{:S(2)}) %collective-permute-start.16) | collective-permute-done | bytes 131104 | tf_op jit(solution)/shard_map/ppermute | solution.py:385
  58.6 1.3 %collective-permute-done.15 = f32[2,128,128]{2,1,0:T(8,128)S(1)} collective-permute-done((f32[2,128,128]{2,1,0:T(8,128)S(1)}, f32[2,128,128]{2,1,0:T(8,128)S(1)}, u32[]{:S(2)}, u32[]{:S(2)}) %collective-permute-start.15) | collective-permute-done | bytes 131104 | tf_op jit(solution)/shard_map/ppermute | solution.py:385
  59.9 2.5 %collective-permute-start.23 = (f32[2,128,128]{2,1,0:T(8,128)S(1)}, f32[2,128,128]{2,1,0:T(8,128)S(1)}, u32[]{:S(2)}, u32[]{:S(2)}) collective-permute-start(f32[2,128,128]{2,1,0:T(8,128)S(1)} %add_add_fusion.rest_0_), channel_id=1, source_target_pairs={{0,96},{1,97},{2,98},{3,99},{4,100},{5,101},{6,102},{7,103},{8,104... | collective-permute-start | bytes 393224 | tf_op jit(solution)/shard_map/ppermute | solution.py:385
  62.4 1.4 %collective-permute-start.21 = (f32[2,128,128]{2,1,0:T(8,128)S(1)}, f32[2,128,128]{2,1,0:T(8,128)S(1)}, u32[]{:S(2)}, u32[]{:S(2)}) collective-permute-start(f32[2,128,128]{2,1,0:T(8,128)S(1)} %add_add_fusion.rest_0_), channel_id=1, source_target_pairs={{0,64},{1,65},{2,66},{3,67},{4,68},{5,69},{6,70},{7,71},{8,72},{9,... | collective-permute-start | bytes 393224 | tf_op jit(solution)/shard_map/ppermute | solution.py:385
  63.7 3.5 %collective-permute-start.18 = (f32[2,128,128]{2,1,0:T(8,128)S(1)}, f32[2,128,128]{2,1,0:T(8,128)S(1)}, u32[]{:S(2)}, u32[]{:S(2)}) collective-permute-start(f32[2,128,128]{2,1,0:T(8,128)S(1)} %add_add_fusion.rest_0_), channel_id=1, source_target_pairs={{0,8},{8,0},{1,9},{9,1},{2,10},{10,2},{3,11},{11,3},{4,12},{12,4},... | collective-permute-start | bytes 393224 | tf_op jit(solution)/shard_map/ppermute | solution.py:389
  67.3 2.3 %collective-permute-start.24 = (f32[2,128,128]{2,1,0:T(8,128)S(1)}, f32[2,128,128]{2,1,0:T(8,128)S(1)}, u32[]{:S(2)}, u32[]{:S(2)}) collective-permute-start(f32[2,128,128]{2,1,0:T(8,128)S(1)} %collective-permute-done.23.rest_6_), channel_id=1, source_target_pairs={{0,8},{8,0},{1,9},{9,1},{2,10},{10,2},{3,11},{11,3},{4,12},{12,4},... | collective-permute-start | bytes 393224 | tf_op jit(solution)/shard_map/ppermute | solution.py:389
  69.6 2.5 %collective-permute-start.22 = (f32[2,128,128]{2,1,0:T(8,128)S(1)}, f32[2,128,128]{2,1,0:T(8,128)S(1)}, u32[]{:S(2)}, u32[]{:S(2)}) collective-permute-start(f32[2,128,128]{2,1,0:T(8,128)S(1)} %collective-permute-done.21.rest_4_), channel_id=1, source_target_pairs={{0,8},{8,0},{1,9},{9,1},{2,10},{10,2},{3,11},{11,3},{4,12},{12,4},... | collective-permute-start | bytes 393224 | tf_op jit(solution)/shard_map/ppermute | solution.py:389
  72.1 1.4 %collective-permute-start.20 = (f32[2,128,128]{2,1,0:T(8,128)S(1)}, f32[2,128,128]{2,1,0:T(8,128)S(1)}, u32[]{:S(2)}, u32[]{:S(2)}) collective-permute-start(f32[2,128,128]{2,1,0:T(8,128)S(1)} %collective-permute-done.19.rest_2_), channel_id=1, source_target_pairs={{0,8},{8,0},{1,9},{9,1},{2,10},{10,2},{3,11},{11,3},{4,12},{12,4},... | collective-permute-start | bytes 393224 | tf_op jit(solution)/shard_map/ppermute | solution.py:389
  74.5 4.4 %update_8.1 = (bf16[1024,1792]{1,0:T(8,128)(2,1)}, bf16[1024,1792]{1,0:T(8,128)(2,1)}, f32[1024,128]{1,0:T(8,128)}, f32[1024,128]{1,0:T(8,128)}, f32[1024,128]{1,0:T(8,128)}, /*index=5*/f32[1024,128]{1,0:T(8,128)}) custom-call(bf16[2,128,1792]{2,1,0:T(8,128)(2,1)S(1)} %basis_columns.1.basis_ref, f32[1024,128]{1,0:T(8,128)S(1)} %copy-done.3, ...), custom_call_target="tpu_custom_call" | custom-call | flops 3200000000 | bytes 8000000 | tf_op jit(solution)/shard_map/update_8/pallas_call | solution.py:353
  (50 shorter events, 9.8 us)
Async XLA Ops:
  2.6 5.1 %collective-permute-start.2 = (f32[128,1024]{1,0:T(8,128)S(1)}, f32[128,1024]{1,0:T(8,128)S(1)}, u32[]{:S(2)}, u32[]{:S(2)}) collective-permute-start(f32[128,1024]{1,0:T(8,128)S(1)} %get-tuple-element.28), channel_id=1, source_target_pairs={{0,8},{8,0},{1,9},{9,1},{2,10},{10,2},{3,11},{11,3},{4,12},{12,4},... | collective-permute-start | bytes 1572872 | tf_op jit(solution)/shard_map/ppermute | solution.py:389
  4.1 4.6 %collective-permute-start = (f32[128,1024]{1,0:T(8,128)S(1)}, f32[128,1024]{1,0:T(8,128)S(1)}, u32[]{:S(2)}, u32[]{:S(2)}) collective-permute-start(f32[128,1024]{1,0:T(8,128)S(1)} %get-tuple-element.26), channel_id=1, source_target_pairs={{0,8},{8,0},{1,9},{9,1},{2,10},{10,2},{3,11},{11,3},{4,12},{12,4},... | collective-permute-start | bytes 1572872 | tf_op jit(solution)/shard_map/ppermute | solution.py:389
  4.2 5.4 %collective-permute-start.1 = (f32[128,1024]{1,0:T(8,128)S(1)}, f32[128,1024]{1,0:T(8,128)S(1)}, u32[]{:S(2)}, u32[]{:S(2)}) collective-permute-start(f32[128,1024]{1,0:T(8,128)S(1)} %get-tuple-element.27), channel_id=1, source_target_pairs={{0,8},{8,0},{1,9},{9,1},{2,10},{10,2},{3,11},{11,3},{4,12},{12,4},... | collective-permute-start | bytes 1572872 | tf_op jit(solution)/shard_map/ppermute | solution.py:389
  4.6 4.9 %collective-permute-start.3 = (f32[128,1024]{1,0:T(8,128)S(1)}, f32[128,1024]{1,0:T(8,128)S(1)}, u32[]{:S(2)}, u32[]{:S(2)}) collective-permute-start(f32[128,1024]{1,0:T(8,128)S(1)} %get-tuple-element.29), channel_id=1, source_target_pairs={{0,8},{8,0},{1,9},{9,1},{2,10},{10,2},{3,11},{11,3},{4,12},{12,4},... | collective-permute-start | bytes 1572872 | tf_op jit(solution)/shard_map/ppermute | solution.py:389
  4.7 23.8 %collective-permute-start.5 = (f32[128,1024]{1,0:T(8,128)S(1)}, f32[128,1024]{1,0:T(8,128)S(1)}, u32[]{:S(2)}, u32[]{:S(2)}) collective-permute-start(f32[128,1024]{1,0:T(8,128)S(1)} %get-tuple-element.32), channel_id=1, source_target_pairs={{0,64},{1,65},{2,66},{3,67},{4,68},{5,69},{6,70},{7,71},{8,10},{9,... | collective-permute-start | bytes 1572872 | tf_op jit(solution)/shard_map/ppermute | solution.py:385
  7.8 24.1 %collective-permute-start.7 = (f32[256,1024]{1,0:T(8,128)S(1)}, f32[256,1024]{1,0:T(8,128)S(1)}, u32[]{:S(2)}, u32[]{:S(2)}) collective-permute-start(f32[256,1024]{1,0:T(8,128)S(1)} %pair_3.1), channel_id=1, source_target_pairs={{0,96},{1,97},{2,98},{3,99},{4,100},{5,101},{6,102},{7,103},{8,11}... | collective-permute-start | bytes 3145736 | tf_op jit(solution)/shard_map/ppermute | solution.py:385
  8.8 23.1 %collective-permute-start.6 = (f32[256,1024]{1,0:T(8,128)S(1)}, f32[256,1024]{1,0:T(8,128)S(1)}, u32[]{:S(2)}, u32[]{:S(2)}) collective-permute-start(f32[256,1024]{1,0:T(8,128)S(1)} %pair_1.1), channel_id=1, source_target_pairs={{0,32},{1,33},{2,34},{3,35},{4,36},{5,37},{6,38},{7,39},{8,9},{9,1... | collective-permute-start | bytes 3145736 | tf_op jit(solution)/shard_map/ppermute | solution.py:385
  9.5 28.8 %collective-permute-start.8 = (f32[128,1024]{1,0:T(8,128)S(1)}, f32[128,1024]{1,0:T(8,128)S(1)}, u32[]{:S(2)}, u32[]{:S(2)}) collective-permute-start(f32[128,1024]{1,0:T(8,128)S(1)} %collective-permute-done.1), channel_id=1, source_target_pairs={{0,64},{1,65},{2,66},{3,67},{4,68},{5,69},{6,70},{7,71},{8,10},{9,... | collective-permute-start | bytes 1572872 | tf_op jit(solution)/shard_map/ppermute | solution.py:385
  28.5 7.1 %collective-permute-start.10 = (f32[2,2,128,128]{3,2,1,0:T(8,128)S(1)}, f32[2,2,128,128]{3,2,1,0:T(8,128)S(1)}, u32[]{:S(2)}, u32[]{:S(2)}) collective-permute-start(f32[2,2,128,128]{3,2,1,0:T(8,128)S(1)} %pad_maximum_fusion.rest_5_), channel_id=1, source_target_pairs={{0,64},{1,65},{2,66},{3,67},{4,68},{5,69},{6,70},{7,71},{8,10},{9,... | collective-permute-start | bytes 786440 | tf_op jit(solution)/shard_map/ppermute | solution.py:385
  31.5 6.9 %collective-permute-start.9 = (f32[2,2,128,128]{3,2,1,0:T(8,128)S(1)}, f32[2,2,128,128]{3,2,1,0:T(8,128)S(1)}, u32[]{:S(2)}, u32[]{:S(2)}) collective-permute-start(f32[2,2,128,128]{3,2,1,0:T(8,128)S(1)} %pad_maximum_fusion.rest_5_), channel_id=1, source_target_pairs={{0,32},{1,33},{2,34},{3,35},{4,36},{5,37},{6,38},{7,39},{8,9},{9,1... | collective-permute-start | bytes 786440 | tf_op jit(solution)/shard_map/ppermute | solution.py:385
  31.9 6.9 %collective-permute-start.11 = (f32[2,2,128,128]{3,2,1,0:T(8,128)S(1)}, f32[2,2,128,128]{3,2,1,0:T(8,128)S(1)}, u32[]{:S(2)}, u32[]{:S(2)}) collective-permute-start(f32[2,2,128,128]{3,2,1,0:T(8,128)S(1)} %pad_maximum_fusion.rest_5_), channel_id=1, source_target_pairs={{0,96},{1,97},{2,98},{3,99},{4,100},{5,101},{6,102},{7,103},{8,11}... | collective-permute-start | bytes 786440 | tf_op jit(solution)/shard_map/ppermute | solution.py:385
  39.7 7.3 %collective-permute-start.12 = (f32[2,2,128,128]{3,2,1,0:T(8,128)S(1)}, f32[2,2,128,128]{3,2,1,0:T(8,128)S(1)}, u32[]{:S(2)}, u32[]{:S(2)}) collective-permute-start(f32[2,2,128,128]{3,2,1,0:T(8,128)S(1)} %get-tuple-element.41), channel_id=1, source_target_pairs={{0,2},{1,3},{2,0},{3,1},{4,6},{5,7},{6,4},{7,5},{8,72},{9,73},{10,... | collective-permute-start | bytes 786440 | tf_op jit(solution)/shard_map/ppermute | solution.py:385
  42.3 7.5 %collective-permute-start.13 = (f32[2,2,128,128]{3,2,1,0:T(8,128)S(1)}, f32[2,2,128,128]{3,2,1,0:T(8,128)S(1)}, u32[]{:S(2)}, u32[]{:S(2)}) collective-permute-start(f32[2,2,128,128]{3,2,1,0:T(8,128)S(1)} %get-tuple-element.42), channel_id=1, source_target_pairs={{0,1},{1,2},{2,3},{3,0},{4,5},{5,6},{6,7},{7,4},{8,40},{9,41},{10,... | collective-permute-start | bytes 786440 | tf_op jit(solution)/shard_map/ppermute | solution.py:385
  42.6 7.2 %collective-permute-start.14 = (f32[2,2,128,128]{3,2,1,0:T(8,128)S(1)}, f32[2,2,128,128]{3,2,1,0:T(8,128)S(1)}, u32[]{:S(2)}, u32[]{:S(2)}) collective-permute-start(f32[2,2,128,128]{3,2,1,0:T(8,128)S(1)} %get-tuple-element.43), channel_id=1, source_target_pairs={{0,3},{1,0},{2,1},{3,2},{4,7},{5,4},{6,5},{7,6},{8,104},{9,105},{1... | collective-permute-start | bytes 786440 | tf_op jit(solution)/shard_map/ppermute | solution.py:385
  49.8 6.0 %collective-permute-start.17 = (f32[2,128,128]{2,1,0:T(8,128)S(1)}, f32[2,128,128]{2,1,0:T(8,128)S(1)}, u32[]{:S(2)}, u32[]{:S(2)}) collective-permute-start(f32[2,128,128]{2,1,0:T(8,128)S(1)} %get-tuple-element.44), channel_id=1, source_target_pairs={{0,16},{1,17},{2,18},{3,19},{4,20},{5,21},{6,22},{7,23},{8,24},{9,... | collective-permute-start | bytes 393224 | tf_op jit(solution)/shard_map/ppermute | solution.py:385
  53.5 5.1 %collective-permute-start.16 = (f32[2,128,128]{2,1,0:T(8,128)S(1)}, f32[2,128,128]{2,1,0:T(8,128)S(1)}, u32[]{:S(2)}, u32[]{:S(2)}) collective-permute-start(f32[2,128,128]{2,1,0:T(8,128)S(1)} %get-tuple-element.45), channel_id=1, source_target_pairs={{0,20},{1,21},{2,22},{3,23},{4,0},{5,1},{6,2},{7,3},{8,28},{9,29},... | collective-permute-start | bytes 393224 | tf_op jit(solution)/shard_map/ppermute | solution.py:385
  53.9 5.9 %collective-permute-start.15 = (f32[2,128,128]{2,1,0:T(8,128)S(1)}, f32[2,128,128]{2,1,0:T(8,128)S(1)}, u32[]{:S(2)}, u32[]{:S(2)}) collective-permute-start(f32[2,128,128]{2,1,0:T(8,128)S(1)} %get-tuple-element.45), channel_id=1, source_target_pairs={{0,4},{1,5},{2,6},{3,7},{4,16},{5,17},{6,18},{7,19},{8,12},{9,13},... | collective-permute-start | bytes 393224 | tf_op jit(solution)/shard_map/ppermute | solution.py:385
  59.9 7.4 %collective-permute-start.23 = (f32[2,128,128]{2,1,0:T(8,128)S(1)}, f32[2,128,128]{2,1,0:T(8,128)S(1)}, u32[]{:S(2)}, u32[]{:S(2)}) collective-permute-start(f32[2,128,128]{2,1,0:T(8,128)S(1)} %add_add_fusion.rest_0_), channel_id=1, source_target_pairs={{0,96},{1,97},{2,98},{3,99},{4,100},{5,101},{6,102},{7,103},{8,104... | collective-permute-start | bytes 393224 | tf_op jit(solution)/shard_map/ppermute | solution.py:385
  62.4 7.2 %collective-permute-start.21 = (f32[2,128,128]{2,1,0:T(8,128)S(1)}, f32[2,128,128]{2,1,0:T(8,128)S(1)}, u32[]{:S(2)}, u32[]{:S(2)}) collective-permute-start(f32[2,128,128]{2,1,0:T(8,128)S(1)} %add_add_fusion.rest_0_), channel_id=1, source_target_pairs={{0,64},{1,65},{2,66},{3,67},{4,68},{5,69},{6,70},{7,71},{8,72},{9,... | collective-permute-start | bytes 393224 | tf_op jit(solution)/shard_map/ppermute | solution.py:385
  63.7 8.4 %collective-permute-start.19 = (f32[2,128,128]{2,1,0:T(8,128)S(1)}, f32[2,128,128]{2,1,0:T(8,128)S(1)}, u32[]{:S(2)}, u32[]{:S(2)}) collective-permute-start(f32[2,128,128]{2,1,0:T(8,128)S(1)} %add_add_fusion.rest_0_), channel_id=1, source_target_pairs={{0,32},{1,33},{2,34},{3,35},{4,36},{5,37},{6,38},{7,39},{8,40},{9,... | collective-permute-start | bytes 393224 | tf_op jit(solution)/shard_map/ppermute | solution.py:385
  63.7 9.8 %collective-permute-start.18 = (f32[2,128,128]{2,1,0:T(8,128)S(1)}, f32[2,128,128]{2,1,0:T(8,128)S(1)}, u32[]{:S(2)}, u32[]{:S(2)}) collective-permute-start(f32[2,128,128]{2,1,0:T(8,128)S(1)} %add_add_fusion.rest_0_), channel_id=1, source_target_pairs={{0,8},{8,0},{1,9},{9,1},{2,10},{10,2},{3,11},{11,3},{4,12},{12,4},... | collective-permute-start | bytes 393224 | tf_op jit(solution)/shard_map/ppermute | solution.py:389
  67.3 6.3 %collective-permute-start.24 = (f32[2,128,128]{2,1,0:T(8,128)S(1)}, f32[2,128,128]{2,1,0:T(8,128)S(1)}, u32[]{:S(2)}, u32[]{:S(2)}) collective-permute-start(f32[2,128,128]{2,1,0:T(8,128)S(1)} %collective-permute-done.23.rest_6_), channel_id=1, source_target_pairs={{0,8},{8,0},{1,9},{9,1},{2,10},{10,2},{3,11},{11,3},{4,12},{12,4},... | collective-permute-start | bytes 393224 | tf_op jit(solution)/shard_map/ppermute | solution.py:389
  69.6 4.0 %collective-permute-start.22 = (f32[2,128,128]{2,1,0:T(8,128)S(1)}, f32[2,128,128]{2,1,0:T(8,128)S(1)}, u32[]{:S(2)}, u32[]{:S(2)}) collective-permute-start(f32[2,128,128]{2,1,0:T(8,128)S(1)} %collective-permute-done.21.rest_4_), channel_id=1, source_target_pairs={{0,8},{8,0},{1,9},{9,1},{2,10},{10,2},{3,11},{11,3},{4,12},{12,4},... | collective-permute-start | bytes 393224 | tf_op jit(solution)/shard_map/ppermute | solution.py:389
  72.1 2.4 %collective-permute-start.20 = (f32[2,128,128]{2,1,0:T(8,128)S(1)}, f32[2,128,128]{2,1,0:T(8,128)S(1)}, u32[]{:S(2)}, u32[]{:S(2)}) collective-permute-start(f32[2,128,128]{2,1,0:T(8,128)S(1)} %collective-permute-done.19.rest_2_), channel_id=1, source_target_pairs={{0,8},{8,0},{1,9},{9,1},{2,10},{10,2},{3,11},{11,3},{4,12},{12,4},... | collective-permute-start | bytes 393224 | tf_op jit(solution)/shard_map/ppermute | solution.py:389
  (8 other events, 223.8 us)

commit v4 on v3

--- a/solution.py
+++ b/solution.py
@@ -435,7 +435,7 @@
         send(done, lambda x, z, c, y, k=k: (x + k, z, c, y)) for k in range(1, 4)
     ]
     moments = (gate_first, gate_second, up_first, up_second)
-    places = tuple((k, other) for k in range(4) for other in (False, True))
+    places = tuple((k, other) for k in (0, 2, 3, 1) for other in (False, True))
     grads = [swap_core(own[k]) if other else own[k] for k, other in places]
     outs = update(basis, moments, grads, places)
     gate_step, up_step, gfn, gsn, ufn, usn = outs

time: 79.2 us -> 78.3 us (0.989)
  starting transfers between devices: 38.5 us -> 37.5 us
    ppermute x9, starting transfers between devices: 12.6 us -> 11.3 us  [swap_core(): return lax.ppermute(value, 'core', [(0, 1), (1, 0)])]
where the time goes in v4:
time: 78.3 us; the launch traced here: 78.2 us
  starting transfers between devices  37.5 us (48%)
  Pallas kernels  23 us (29%)
  waiting for transfers between devices  15 us (19%)
  local copies, waits for them, and re-layouts  1.62 us (2%)
  between operations  0.93 us (1%)
    ppermute x16, starting transfers between devices, send(): return lax.ppermute(value, AXES, perm)  26.2 us
    pallas_call x1, Pallas kernels, reduce_both(): pl.pallas_call(reduce_kernel, in_specs=[pl.BlockSpec(memory_space=pltpu.S...  15.8 us
    ppermute x16, waiting for transfers between devices, send(): return lax.ppermute(value, AXES, perm)  13 us
    ppermute x9, starting transfers between devices, swap_core(): return lax.ppermute(value, 'core', [(0, 1), (1, 0)])  11.3 us
    pallas_call x1, Pallas kernels, update(): pl.pallas_call(functools.partial(update_kernel, places=places, before=len...  4.41 us
    ppermute x9, waiting for transfers between devices, swap_core(): return lax.ppermute(value, 'core', [(0, 1), (1, 0)])  1.98 us
    unnamed x14, local copies, waits for them, and re-layouts  1.62 us
  transfers between devices with their start and end apart: 25, of which 10 were waited for; matrix products, arithmetic and copies ran while one was open for 0% of the time, Pallas kernels for 22%

profile of v4, /device:TPU:1, one launch (start us, length us, event | category | flops | bytes accessed | tf_op | source)
XLA Modules:
  0.0 78.2 jit_solution(13976596311620086706)
XLA Ops:
  0.6 1.6 %copy-done = bf16[128,8192]{1,0:T(8,128)(2,1)S(1)} copy-done((bf16[128,8192]{1,0:T(8,128)(2,1)S(1)}, bf16[128,8192]{1,0:T(8,128)(2,1)}, u32[]{:S(2)}) %copy-start) | copy-done | bytes 2097176
  2.6 1.5 %collective-permute-start.2 = (f32[128,1024]{1,0:T(8,128)S(1)}, f32[128,1024]{1,0:T(8,128)S(1)}, u32[]{:S(2)}, u32[]{:S(2)}) collective-permute-start(f32[128,1024]{1,0:T(8,128)S(1)} %get-tuple-element.28), channel_id=1, source_target_pairs={{0,8},{8,0},{1,9},{9,1},{2,10},{10,2},{3,11},{11,3},{4,12},{12,4},... | collective-permute-start | bytes 1572872 | tf_op jit(solution)/shard_map/ppermute | solution.py:389
  4.7 3.0 %collective-permute-start.5 = (f32[128,1024]{1,0:T(8,128)S(1)}, f32[128,1024]{1,0:T(8,128)S(1)}, u32[]{:S(2)}, u32[]{:S(2)}) collective-permute-start(f32[128,1024]{1,0:T(8,128)S(1)} %get-tuple-element.32), channel_id=1, source_target_pairs={{0,64},{1,65},{2,66},{3,67},{4,68},{5,69},{6,70},{7,71},{8,10},{9,... | collective-permute-start | bytes 1572872 | tf_op jit(solution)/shard_map/ppermute | solution.py:385
  9.5 1.3 %collective-permute-start.8 = (f32[128,1024]{1,0:T(8,128)S(1)}, f32[128,1024]{1,0:T(8,128)S(1)}, u32[]{:S(2)}, u32[]{:S(2)}) collective-permute-start(f32[128,1024]{1,0:T(8,128)S(1)} %collective-permute-done.1), channel_id=1, source_target_pairs={{0,64},{1,65},{2,66},{3,67},{4,68},{5,69},{6,70},{7,71},{8,10},{9,... | collective-permute-start | bytes 1572872 | tf_op jit(solution)/shard_map/ppermute | solution.py:385
  10.9 15.8 %reduce_both.1 = f32[2,128,128]{2,1,0:T(8,128)S(1)} custom-call(s32[2]{0:T(128)S(1)} %copy-done.2, bf16[128,28672]{1,0:T(8,128)(2,1)} %gate_hbm.1, bf16[128,28672]{1,0:T(8,128)(2,1)} %up_hbm.1), custom_call_target="tpu_custom_call" | custom-call | flops 9395240960 | bytes 14680064 | tf_op jit(solution)/shard_map/reduce_both/pallas_call | solution.py:134
  27.4 1.0 %collective-permute-done.4 = f32[2,128,128]{2,1,0:T(8,128)S(1)} collective-permute-done((f32[2,128,128]{2,1,0:T(8,128)S(1)}, f32[2,128,128]{2,1,0:T(8,128)S(1)}, u32[]{:S(2)}, u32[]{:S(2)}) %collective-permute-start.4) | collective-permute-done | bytes 131104 | tf_op jit(solution)/shard_map/ppermute | solution.py:389
  28.5 3.0 %collective-permute-start.10 = (f32[2,2,128,128]{3,2,1,0:T(8,128)S(1)}, f32[2,2,128,128]{3,2,1,0:T(8,128)S(1)}, u32[]{:S(2)}, u32[]{:S(2)}) collective-permute-start(f32[2,2,128,128]{3,2,1,0:T(8,128)S(1)} %pad_maximum_fusion.rest_5_), channel_id=1, source_target_pairs={{0,64},{1,65},{2,66},{3,67},{4,68},{5,69},{6,70},{7,71},{8,10},{9,... | collective-permute-start | bytes 786440 | tf_op jit(solution)/shard_map/ppermute | solution.py:385
  31.9 2.3 %collective-permute-start.11 = (f32[2,2,128,128]{3,2,1,0:T(8,128)S(1)}, f32[2,2,128,128]{3,2,1,0:T(8,128)S(1)}, u32[]{:S(2)}, u32[]{:S(2)}) collective-permute-start(f32[2,2,128,128]{3,2,1,0:T(8,128)S(1)} %pad_maximum_fusion.rest_5_), channel_id=1, source_target_pairs={{0,96},{1,97},{2,98},{3,99},{4,100},{5,101},{6,102},{7,103},{8,11}... | collective-permute-start | bytes 786440 | tf_op jit(solution)/shard_map/ppermute | solution.py:385
  34.1 1.4 %collective-permute-done.10.rest_7_ = f32[2,2,128,128]{3,2,1,0:T(8,128)S(1)} collective-permute-done((f32[2,2,128,128]{3,2,1,0:T(8,128)S(1)}, f32[2,2,128,128]{3,2,1,0:T(8,128)S(1)}, u32[]{:S(2)}, u32[]{:S(2)}) %collective-permute-start.10) | collective-permute-done | bytes 262176 | tf_op jit(solution)/shard_map/ppermute | solution.py:385
  35.6 2.8 %collective-permute-done.9.rest_6_ = f32[2,2,128,128]{3,2,1,0:T(8,128)S(1)} collective-permute-done((f32[2,2,128,128]{3,2,1,0:T(8,128)S(1)}, f32[2,2,128,128]{3,2,1,0:T(8,128)S(1)}, u32[]{:S(2)}, u32[]{:S(2)}) %collective-permute-start.9) | collective-permute-done | bytes 262176 | tf_op jit(solution)/shard_map/ppermute | solution.py:385
  39.7 2.6 %collective-permute-start.12 = (f32[2,2,128,128]{3,2,1,0:T(8,128)S(1)}, f32[2,2,128,128]{3,2,1,0:T(8,128)S(1)}, u32[]{:S(2)}, u32[]{:S(2)}) collective-permute-start(f32[2,2,128,128]{3,2,1,0:T(8,128)S(1)} %get-tuple-element.41), channel_id=1, source_target_pairs={{0,2},{1,3},{2,0},{3,1},{4,6},{5,7},{6,4},{7,5},{8,72},{9,73},{10,... | collective-permute-start | bytes 786440 | tf_op jit(solution)/shard_map/ppermute | solution.py:385
  42.6 2.3 %collective-permute-start.14 = (f32[2,2,128,128]{3,2,1,0:T(8,128)S(1)}, f32[2,2,128,128]{3,2,1,0:T(8,128)S(1)}, u32[]{:S(2)}, u32[]{:S(2)}) collective-permute-start(f32[2,2,128,128]{3,2,1,0:T(8,128)S(1)} %get-tuple-element.43), channel_id=1, source_target_pairs={{0,3},{1,0},{2,1},{3,2},{4,7},{5,4},{6,5},{7,6},{8,104},{9,105},{1... | collective-permute-start | bytes 786440 | tf_op jit(solution)/shard_map/ppermute | solution.py:385
  45.0 1.2 %basis_columns.1.basis_ref = bf16[2,128,1792]{2,1,0:T(8,128)(2,1)S(1)} custom-call(s32[2]{0:T(128)S(1)} %copy-done.2), custom_call_target="tpu_custom_call" | custom-call | flops 9175040 | bytes 917504 | tf_op jit(solution)/shard_map/basis_columns/pallas_call | solution.py:293
  47.0 2.8 %collective-permute-done.13.refs_2_ = f32[2,2,128,128]{3,2,1,0:T(8,128)S(1)} collective-permute-done((f32[2,2,128,128]{3,2,1,0:T(8,128)S(1)}, f32[2,2,128,128]{3,2,1,0:T(8,128)S(1)}, u32[]{:S(2)}, u32[]{:S(2)}) %collective-permute-start.13) | collective-permute-done | bytes 262176 | tf_op jit(solution)/shard_map/ppermute | solution.py:385
  49.8 3.7 %collective-permute-start.17 = (f32[2,128,128]{2,1,0:T(8,128)S(1)}, f32[2,128,128]{2,1,0:T(8,128)S(1)}, u32[]{:S(2)}, u32[]{:S(2)}) collective-permute-start(f32[2,128,128]{2,1,0:T(8,128)S(1)} %get-tuple-element.44), channel_id=1, source_target_pairs={{0,16},{1,17},{2,18},{3,19},{4,20},{5,21},{6,22},{7,23},{8,24},{9,... | collective-permute-start | bytes 393224 | tf_op jit(solution)/shard_map/ppermute | solution.py:385
  53.9 1.0 %collective-permute-start.15 = (f32[2,128,128]{2,1,0:T(8,128)S(1)}, f32[2,128,128]{2,1,0:T(8,128)S(1)}, u32[]{:S(2)}, u32[]{:S(2)}) collective-permute-start(f32[2,128,128]{2,1,0:T(8,128)S(1)} %get-tuple-element.45), channel_id=1, source_target_pairs={{0,4},{1,5},{2,6},{3,7},{4,16},{5,17},{6,18},{7,19},{8,12},{9,13},... | collective-permute-start | bytes 393224 | tf_op jit(solution)/shard_map/ppermute | solution.py:385
  55.9 2.7 %collective-permute-done.16 = f32[2,128,128]{2,1,0:T(8,128)S(1)} collective-permute-done((f32[2,128,128]{2,1,0:T(8,128)S(1)}, f32[2,128,128]{2,1,0:T(8,128)S(1)}, u32[]{:S(2)}, u32[]{:S(2)}) %collective-permute-start.16) | collective-permute-done | bytes 131104 | tf_op jit(solution)/shard_map/ppermute | solution.py:385
  58.6 1.3 %collective-permute-done.15 = f32[2,128,128]{2,1,0:T(8,128)S(1)} collective-permute-done((f32[2,128,128]{2,1,0:T(8,128)S(1)}, f32[2,128,128]{2,1,0:T(8,128)S(1)}, u32[]{:S(2)}, u32[]{:S(2)}) %collective-permute-start.15) | collective-permute-done | bytes 131104 | tf_op jit(solution)/shard_map/ppermute | solution.py:385
  59.9 2.1 %collective-permute-start.23 = (f32[2,128,128]{2,1,0:T(8,128)S(1)}, f32[2,128,128]{2,1,0:T(8,128)S(1)}, u32[]{:S(2)}, u32[]{:S(2)}) collective-permute-start(f32[2,128,128]{2,1,0:T(8,128)S(1)} %add_add_fusion.rest_0_), channel_id=1, source_target_pairs={{0,32},{1,33},{2,34},{3,35},{4,36},{5,37},{6,38},{7,39},{8,40},{9,... | collective-permute-start | bytes 393224 | tf_op jit(solution)/shard_map/ppermute | solution.py:385
  62.6 1.5 %collective-permute-start.19 = (f32[2,128,128]{2,1,0:T(8,128)S(1)}, f32[2,128,128]{2,1,0:T(8,128)S(1)}, u32[]{:S(2)}, u32[]{:S(2)}) collective-permute-start(f32[2,128,128]{2,1,0:T(8,128)S(1)} %add_add_fusion.rest_0_), channel_id=1, source_target_pairs={{0,64},{1,65},{2,66},{3,67},{4,68},{5,69},{6,70},{7,71},{8,72},{9,... | collective-permute-start | bytes 393224 | tf_op jit(solution)/shard_map/ppermute | solution.py:385
  64.1 3.8 %collective-permute-start.18 = (f32[2,128,128]{2,1,0:T(8,128)S(1)}, f32[2,128,128]{2,1,0:T(8,128)S(1)}, u32[]{:S(2)}, u32[]{:S(2)}) collective-permute-start(f32[2,128,128]{2,1,0:T(8,128)S(1)} %add_add_fusion.rest_0_), channel_id=1, source_target_pairs={{0,8},{8,0},{1,9},{9,1},{2,10},{10,2},{3,11},{11,3},{4,12},{12,4},... | collective-permute-start | bytes 393224 | tf_op jit(solution)/shard_map/ppermute | solution.py:389
  67.9 2.2 %collective-permute-start.24 = (f32[2,128,128]{2,1,0:T(8,128)S(1)}, f32[2,128,128]{2,1,0:T(8,128)S(1)}, u32[]{:S(2)}, u32[]{:S(2)}) collective-permute-start(f32[2,128,128]{2,1,0:T(8,128)S(1)} %collective-permute-done.23.rest_6_), channel_id=1, source_target_pairs={{0,8},{8,0},{1,9},{9,1},{2,10},{10,2},{3,11},{11,3},{4,12},{12,4},... | collective-permute-start | bytes 393224 | tf_op jit(solution)/shard_map/ppermute | solution.py:389
  70.1 2.4 %collective-permute-start.20 = (f32[2,128,128]{2,1,0:T(8,128)S(1)}, f32[2,128,128]{2,1,0:T(8,128)S(1)}, u32[]{:S(2)}, u32[]{:S(2)}) collective-permute-start(f32[2,128,128]{2,1,0:T(8,128)S(1)} %collective-permute-done.19.rest_2_), channel_id=1, source_target_pairs={{0,8},{8,0},{1,9},{9,1},{2,10},{10,2},{3,11},{11,3},{4,12},{12,4},... | collective-permute-start | bytes 393224 | tf_op jit(solution)/shard_map/ppermute | solution.py:389
  73.6 4.4 %update_8.1 = (bf16[1024,1792]{1,0:T(8,128)(2,1)}, bf16[1024,1792]{1,0:T(8,128)(2,1)}, f32[1024,128]{1,0:T(8,128)}, f32[1024,128]{1,0:T(8,128)}, f32[1024,128]{1,0:T(8,128)}, /*index=5*/f32[1024,128]{1,0:T(8,128)}) custom-call(bf16[2,128,1792]{2,1,0:T(8,128)(2,1)S(1)} %basis_columns.1.basis_ref, f32[1024,128]{1,0:T(8,128)S(1)} %copy-done.3, ...), custom_call_target="tpu_custom_call" | custom-call | flops 3200000000 | bytes 8000000 | tf_op jit(solution)/shard_map/update_8/pallas_call | solution.py:353
  (50 shorter events, 9.5 us)
Async XLA Ops:
  2.6 5.1 %collective-permute-start.2 = (f32[128,1024]{1,0:T(8,128)S(1)}, f32[128,1024]{1,0:T(8,128)S(1)}, u32[]{:S(2)}, u32[]{:S(2)}) collective-permute-start(f32[128,1024]{1,0:T(8,128)S(1)} %get-tuple-element.28), channel_id=1, source_target_pairs={{0,8},{8,0},{1,9},{9,1},{2,10},{10,2},{3,11},{11,3},{4,12},{12,4},... | collective-permute-start | bytes 1572872 | tf_op jit(solution)/shard_map/ppermute | solution.py:389
  4.1 4.6 %collective-permute-start = (f32[128,1024]{1,0:T(8,128)S(1)}, f32[128,1024]{1,0:T(8,128)S(1)}, u32[]{:S(2)}, u32[]{:S(2)}) collective-permute-start(f32[128,1024]{1,0:T(8,128)S(1)} %get-tuple-element.26), channel_id=1, source_target_pairs={{0,8},{8,0},{1,9},{9,1},{2,10},{10,2},{3,11},{11,3},{4,12},{12,4},... | collective-permute-start | bytes 1572872 | tf_op jit(solution)/shard_map/ppermute | solution.py:389
  4.2 5.4 %collective-permute-start.1 = (f32[128,1024]{1,0:T(8,128)S(1)}, f32[128,1024]{1,0:T(8,128)S(1)}, u32[]{:S(2)}, u32[]{:S(2)}) collective-permute-start(f32[128,1024]{1,0:T(8,128)S(1)} %get-tuple-element.27), channel_id=1, source_target_pairs={{0,8},{8,0},{1,9},{9,1},{2,10},{10,2},{3,11},{11,3},{4,12},{12,4},... | collective-permute-start | bytes 1572872 | tf_op jit(solution)/shard_map/ppermute | solution.py:389
  4.6 4.9 %collective-permute-start.3 = (f32[128,1024]{1,0:T(8,128)S(1)}, f32[128,1024]{1,0:T(8,128)S(1)}, u32[]{:S(2)}, u32[]{:S(2)}) collective-permute-start(f32[128,1024]{1,0:T(8,128)S(1)} %get-tuple-element.29), channel_id=1, source_target_pairs={{0,8},{8,0},{1,9},{9,1},{2,10},{10,2},{3,11},{11,3},{4,12},{12,4},... | collective-permute-start | bytes 1572872 | tf_op jit(solution)/shard_map/ppermute | solution.py:389
  4.7 23.8 %collective-permute-start.5 = (f32[128,1024]{1,0:T(8,128)S(1)}, f32[128,1024]{1,0:T(8,128)S(1)}, u32[]{:S(2)}, u32[]{:S(2)}) collective-permute-start(f32[128,1024]{1,0:T(8,128)S(1)} %get-tuple-element.32), channel_id=1, source_target_pairs={{0,64},{1,65},{2,66},{3,67},{4,68},{5,69},{6,70},{7,71},{8,10},{9,... | collective-permute-start | bytes 1572872 | tf_op jit(solution)/shard_map/ppermute | solution.py:385
  7.8 24.1 %collective-permute-start.7 = (f32[256,1024]{1,0:T(8,128)S(1)}, f32[256,1024]{1,0:T(8,128)S(1)}, u32[]{:S(2)}, u32[]{:S(2)}) collective-permute-start(f32[256,1024]{1,0:T(8,128)S(1)} %pair_3.1), channel_id=1, source_target_pairs={{0,96},{1,97},{2,98},{3,99},{4,100},{5,101},{6,102},{7,103},{8,11}... | collective-permute-start | bytes 3145736 | tf_op jit(solution)/shard_map/ppermute | solution.py:385
  8.8 23.1 %collective-permute-start.6 = (f32[256,1024]{1,0:T(8,128)S(1)}, f32[256,1024]{1,0:T(8,128)S(1)}, u32[]{:S(2)}, u32[]{:S(2)}) collective-permute-start(f32[256,1024]{1,0:T(8,128)S(1)} %pair_1.1), channel_id=1, source_target_pairs={{0,32},{1,33},{2,34},{3,35},{4,36},{5,37},{6,38},{7,39},{8,9},{9,1... | collective-permute-start | bytes 3145736 | tf_op jit(solution)/shard_map/ppermute | solution.py:385
  9.5 28.8 %collective-permute-start.8 = (f32[128,1024]{1,0:T(8,128)S(1)}, f32[128,1024]{1,0:T(8,128)S(1)}, u32[]{:S(2)}, u32[]{:S(2)}) collective-permute-start(f32[128,1024]{1,0:T(8,128)S(1)} %collective-permute-done.1), channel_id=1, source_target_pairs={{0,64},{1,65},{2,66},{3,67},{4,68},{5,69},{6,70},{7,71},{8,10},{9,... | collective-permute-start | bytes 1572872 | tf_op jit(solution)/shard_map/ppermute | solution.py:385
  28.5 7.1 %collective-permute-start.10 = (f32[2,2,128,128]{3,2,1,0:T(8,128)S(1)}, f32[2,2,128,128]{3,2,1,0:T(8,128)S(1)}, u32[]{:S(2)}, u32[]{:S(2)}) collective-permute-start(f32[2,2,128,128]{3,2,1,0:T(8,128)S(1)} %pad_maximum_fusion.rest_5_), channel_id=1, source_target_pairs={{0,64},{1,65},{2,66},{3,67},{4,68},{5,69},{6,70},{7,71},{8,10},{9,... | collective-permute-start | bytes 786440 | tf_op jit(solution)/shard_map/ppermute | solution.py:385
  31.5 6.9 %collective-permute-start.9 = (f32[2,2,128,128]{3,2,1,0:T(8,128)S(1)}, f32[2,2,128,128]{3,2,1,0:T(8,128)S(1)}, u32[]{:S(2)}, u32[]{:S(2)}) collective-permute-start(f32[2,2,128,128]{3,2,1,0:T(8,128)S(1)} %pad_maximum_fusion.rest_5_), channel_id=1, source_target_pairs={{0,32},{1,33},{2,34},{3,35},{4,36},{5,37},{6,38},{7,39},{8,9},{9,1... | collective-permute-start | bytes 786440 | tf_op jit(solution)/shard_map/ppermute | solution.py:385
  31.9 6.9 %collective-permute-start.11 = (f32[2,2,128,128]{3,2,1,0:T(8,128)S(1)}, f32[2,2,128,128]{3,2,1,0:T(8,128)S(1)}, u32[]{:S(2)}, u32[]{:S(2)}) collective-permute-start(f32[2,2,128,128]{3,2,1,0:T(8,128)S(1)} %pad_maximum_fusion.rest_5_), channel_id=1, source_target_pairs={{0,96},{1,97},{2,98},{3,99},{4,100},{5,101},{6,102},{7,103},{8,11}... | collective-permute-start | bytes 786440 | tf_op jit(solution)/shard_map/ppermute | solution.py:385
  39.7 7.3 %collective-permute-start.12 = (f32[2,2,128,128]{3,2,1,0:T(8,128)S(1)}, f32[2,2,128,128]{3,2,1,0:T(8,128)S(1)}, u32[]{:S(2)}, u32[]{:S(2)}) collective-permute-start(f32[2,2,128,128]{3,2,1,0:T(8,128)S(1)} %get-tuple-element.41), channel_id=1, source_target_pairs={{0,2},{1,3},{2,0},{3,1},{4,6},{5,7},{6,4},{7,5},{8,72},{9,73},{10,... | collective-permute-start | bytes 786440 | tf_op jit(solution)/shard_map/ppermute | solution.py:385
  42.3 7.5 %collective-permute-start.13 = (f32[2,2,128,128]{3,2,1,0:T(8,128)S(1)}, f32[2,2,128,128]{3,2,1,0:T(8,128)S(1)}, u32[]{:S(2)}, u32[]{:S(2)}) collective-permute-start(f32[2,2,128,128]{3,2,1,0:T(8,128)S(1)} %get-tuple-element.42), channel_id=1, source_target_pairs={{0,1},{1,2},{2,3},{3,0},{4,5},{5,6},{6,7},{7,4},{8,40},{9,41},{10,... | collective-permute-start | bytes 786440 | tf_op jit(solution)/shard_map/ppermute | solution.py:385
  42.6 7.2 %collective-permute-start.14 = (f32[2,2,128,128]{3,2,1,0:T(8,128)S(1)}, f32[2,2,128,128]{3,2,1,0:T(8,128)S(1)}, u32[]{:S(2)}, u32[]{:S(2)}) collective-permute-start(f32[2,2,128,128]{3,2,1,0:T(8,128)S(1)} %get-tuple-element.43), channel_id=1, source_target_pairs={{0,3},{1,0},{2,1},{3,2},{4,7},{5,4},{6,5},{7,6},{8,104},{9,105},{1... | collective-permute-start | bytes 786440 | tf_op jit(solution)/shard_map/ppermute | solution.py:385
  49.8 6.0 %collective-permute-start.17 = (f32[2,128,128]{2,1,0:T(8,128)S(1)}, f32[2,128,128]{2,1,0:T(8,128)S(1)}, u32[]{:S(2)}, u32[]{:S(2)}) collective-permute-start(f32[2,128,128]{2,1,0:T(8,128)S(1)} %get-tuple-element.44), channel_id=1, source_target_pairs={{0,16},{1,17},{2,18},{3,19},{4,20},{5,21},{6,22},{7,23},{8,24},{9,... | collective-permute-start | bytes 393224 | tf_op jit(solution)/shard_map/ppermute | solution.py:385
  53.5 5.1 %collective-permute-start.16 = (f32[2,128,128]{2,1,0:T(8,128)S(1)}, f32[2,128,128]{2,1,0:T(8,128)S(1)}, u32[]{:S(2)}, u32[]{:S(2)}) collective-permute-start(f32[2,128,128]{2,1,0:T(8,128)S(1)} %get-tuple-element.45), channel_id=1, source_target_pairs={{0,20},{1,21},{2,22},{3,23},{4,0},{5,1},{6,2},{7,3},{8,28},{9,29},... | collective-permute-start | bytes 393224 | tf_op jit(solution)/shard_map/ppermute | solution.py:385
  53.9 5.9 %collective-permute-start.15 = (f32[2,128,128]{2,1,0:T(8,128)S(1)}, f32[2,128,128]{2,1,0:T(8,128)S(1)}, u32[]{:S(2)}, u32[]{:S(2)}) collective-permute-start(f32[2,128,128]{2,1,0:T(8,128)S(1)} %get-tuple-element.45), channel_id=1, source_target_pairs={{0,4},{1,5},{2,6},{3,7},{4,16},{5,17},{6,18},{7,19},{8,12},{9,13},... | collective-permute-start | bytes 393224 | tf_op jit(solution)/shard_map/ppermute | solution.py:385
  59.9 8.0 %collective-permute-start.23 = (f32[2,128,128]{2,1,0:T(8,128)S(1)}, f32[2,128,128]{2,1,0:T(8,128)S(1)}, u32[]{:S(2)}, u32[]{:S(2)}) collective-permute-start(f32[2,128,128]{2,1,0:T(8,128)S(1)} %add_add_fusion.rest_0_), channel_id=1, source_target_pairs={{0,32},{1,33},{2,34},{3,35},{4,36},{5,37},{6,38},{7,39},{8,40},{9,... | collective-permute-start | bytes 393224 | tf_op jit(solution)/shard_map/ppermute | solution.py:385
  62.0 8.1 %collective-permute-start.21 = (f32[2,128,128]{2,1,0:T(8,128)S(1)}, f32[2,128,128]{2,1,0:T(8,128)S(1)}, u32[]{:S(2)}, u32[]{:S(2)}) collective-permute-start(f32[2,128,128]{2,1,0:T(8,128)S(1)} %add_add_fusion.rest_0_), channel_id=1, source_target_pairs={{0,96},{1,97},{2,98},{3,99},{4,100},{5,101},{6,102},{7,103},{8,104... | collective-permute-start | bytes 393224 | tf_op jit(solution)/shard_map/ppermute | solution.py:385
  62.6 7.5 %collective-permute-start.19 = (f32[2,128,128]{2,1,0:T(8,128)S(1)}, f32[2,128,128]{2,1,0:T(8,128)S(1)}, u32[]{:S(2)}, u32[]{:S(2)}) collective-permute-start(f32[2,128,128]{2,1,0:T(8,128)S(1)} %add_add_fusion.rest_0_), channel_id=1, source_target_pairs={{0,64},{1,65},{2,66},{3,67},{4,68},{5,69},{6,70},{7,71},{8,72},{9,... | collective-permute-start | bytes 393224 | tf_op jit(solution)/shard_map/ppermute | solution.py:385
  64.1 8.5 %collective-permute-start.18 = (f32[2,128,128]{2,1,0:T(8,128)S(1)}, f32[2,128,128]{2,1,0:T(8,128)S(1)}, u32[]{:S(2)}, u32[]{:S(2)}) collective-permute-start(f32[2,128,128]{2,1,0:T(8,128)S(1)} %add_add_fusion.rest_0_), channel_id=1, source_target_pairs={{0,8},{8,0},{1,9},{9,1},{2,10},{10,2},{3,11},{11,3},{4,12},{12,4},... | collective-permute-start | bytes 393224 | tf_op jit(solution)/shard_map/ppermute | solution.py:389
  67.9 4.7 %collective-permute-start.24 = (f32[2,128,128]{2,1,0:T(8,128)S(1)}, f32[2,128,128]{2,1,0:T(8,128)S(1)}, u32[]{:S(2)}, u32[]{:S(2)}) collective-permute-start(f32[2,128,128]{2,1,0:T(8,128)S(1)} %collective-permute-done.23.rest_6_), channel_id=1, source_target_pairs={{0,8},{8,0},{1,9},{9,1},{2,10},{10,2},{3,11},{11,3},{4,12},{12,4},... | collective-permute-start | bytes 393224 | tf_op jit(solution)/shard_map/ppermute | solution.py:389
  70.0 2.6 %collective-permute-start.22 = (f32[2,128,128]{2,1,0:T(8,128)S(1)}, f32[2,128,128]{2,1,0:T(8,128)S(1)}, u32[]{:S(2)}, u32[]{:S(2)}) collective-permute-start(f32[2,128,128]{2,1,0:T(8,128)S(1)} %collective-permute-done.21.rest_4_), channel_id=1, source_target_pairs={{0,8},{8,0},{1,9},{9,1},{2,10},{10,2},{3,11},{11,3},{4,12},{12,4},... | collective-permute-start | bytes 393224 | tf_op jit(solution)/shard_map/ppermute | solution.py:389
  70.1 3.4 %collective-permute-start.20 = (f32[2,128,128]{2,1,0:T(8,128)S(1)}, f32[2,128,128]{2,1,0:T(8,128)S(1)}, u32[]{:S(2)}, u32[]{:S(2)}) collective-permute-start(f32[2,128,128]{2,1,0:T(8,128)S(1)} %collective-permute-done.19.rest_2_), channel_id=1, source_target_pairs={{0,8},{8,0},{1,9},{9,1},{2,10},{10,2},{3,11},{11,3},{4,12},{12,4},... | collective-permute-start | bytes 393224 | tf_op jit(solution)/shard_map/ppermute | solution.py:389
  (8 other events, 220.0 us)
